TPU v7x, 512 devices: a whole 4x8x8 slice. The times are simulated.
512 devices in a mesh: grp: 8 (over z), seq: 64 (over y, x, core).
Axes of the slice: x: 4, y: 8, z: 8, core: 2. Of those that a mesh axis runs over, the one named last changes fastest.
Arguments:
- kv_states: bfloat16 [8192, 4096], P('seq'), may hold values from -1.5 to 1.5
- queries_t: bfloat16 [2048, 4096], P('seq', 'grp'), may hold values from -6 to 6
- grad_out_t: bfloat16 [2048, 4096], P('seq', 'grp'), may hold values from -48 to 48
- log_norm: float32 [32, 4096], P(None, 'grp'), may hold values from 1.5 to 2.5
- delta: float32 [32, 4096], P(None, 'grp'), may hold values from -48 to 48
- lengths: int32 [16], P('grp'), may hold values from 1 to 256, 3072 in all
Outputs:
- grad_query_t: bfloat16 [2048, 4096], P('seq', 'grp')
- grad_keys: bfloat16 [8192, 2048], P('seq', 'grp')
- grad_values: bfloat16 [8192, 2048], P('seq', 'grp')
Inputs may be any that keep to these rules, and one draw needn't show every extreme that they name: `lengths`: each answer's count of real tokens; one answer is full.
All inputs are finite; a program needn't handle non-finite values. No bound on the sum of `lengths` on one device may be relied on, other than what follows from the above.
Results may differ from a plain program's by a relative error of at most 0.0049.
Values may be sent and summed in bfloat16 or wider, within the bound.
A program may use at most 64 MiB of HBM per device.

v0:
```python
import math

import jax
import jax.numpy as jnp
from jax import lax
from jax.sharding import PartitionSpec as P

HEADS = 32
DH = 64


def from_partner(shard, axis, stride):
    return lax.ppermute(shard, axis, [(i, i ^ 1 << stride) for i in range(lax.axis_size(axis))])


def to_rows(arrived, blocks_h, split, part_rows, per_dev, cols):
    shaped = arrived.reshape(blocks_h, split, part_rows, per_dev, cols)
    shaped = jnp.transpose(shaped, (1, 2, 4, 0, 3))
    return shaped.reshape(split * part_rows, cols * blocks_h * per_dev)


def on_device(kv_states, queries_t, grad_out_t, log_norm, delta, lengths):
    seq_count = lax.axis_size("seq")
    rows = kv_states.shape[0]
    width = 2 * DH
    split = max(1, seq_count // HEADS)
    per_dev = max(1, HEADS // seq_count)
    blocks_h = seq_count // split
    part_rows = rows // split
    keys_all = rows * seq_count
    tokens = queries_t.shape[1]
    local = kv_states.reshape(split, part_rows, width, blocks_h, per_dev)
    local = jnp.transpose(local, (3, 0, 1, 4, 2)).reshape(seq_count, part_rows, per_dev * width)
    arrived = lax.all_to_all(local, "seq", split_axis=0, concat_axis=0, tiled=True)
    key_rows = seq_count * part_rows
    position = lax.axis_index("seq")
    head_block = position // split
    first = position % split == 0
    other_q, other_g = from_partner((queries_t, grad_out_t), "seq", 0)
    q_full = jnp.where(
        first, jnp.concatenate([queries_t, other_q], 0), jnp.concatenate([other_q, queries_t], 0)
    )
    g_full = jnp.where(
        first, jnp.concatenate([grad_out_t, other_g], 0), jnp.concatenate([other_g, grad_out_t], 0)
    )
    q_heads = q_full.reshape(per_dev, DH, tokens)
    g_heads = g_full.reshape(per_dev, DH, tokens)
    norm_rows = lax.dynamic_slice_in_dim(log_norm, head_block * per_dev, per_dev, 0)
    delta_rows = lax.dynamic_slice_in_dim(delta, head_block * per_dev, per_dev, 0)
    answers = lengths.shape[0]
    span = tokens // answers
    place = jnp.arange(tokens, dtype=jnp.int32)
    owner = place // span
    offset = place % span
    table = owner[:, None] == jnp.arange(answers, dtype=jnp.int32)[None, :]
    limit = jnp.sum(jnp.where(table, lengths[None, :], 0), axis=1)
    valid = offset < limit
    block = math.gcd(key_rows, 512)
    count = key_rows // block
    pieces = arrived.reshape(count, block, per_dev, width)

    def step(carry, piece):
        keys_b = piece[..., :DH]
        vals_b = piece[..., DH:]
        scores = jnp.einsum("hdt,khd->htk", q_heads, keys_b, preferred_element_type=jnp.float32)
        probs = (
            jnp.where(valid[None, :, None], jnp.exp(scores - norm_rows[:, :, None]), 0.0) / keys_all
        )
        dprobs = jnp.einsum("hdt,khd->htk", g_heads, vals_b, preferred_element_type=jnp.float32)
        dscores = probs * (dprobs - delta_rows[:, :, None])
        probs_b = probs.astype(jnp.bfloat16)
        dscores_b = dscores.astype(jnp.bfloat16)
        dvals = jnp.einsum("htk,hdt->khd", probs_b, g_heads, preferred_element_type=jnp.float32)
        dkeys = jnp.einsum("htk,hdt->khd", dscores_b, q_heads, preferred_element_type=jnp.float32)
        carry = carry + jnp.einsum(
            "htk,khd->hdt", dscores_b, keys_b, preferred_element_type=jnp.float32
        )
        return (carry, jnp.concatenate([dkeys, dvals], axis=-1))

    start = jnp.zeros((per_dev, DH, tokens), jnp.float32)
    dquery, grads = lax.scan(step, start, pieces)
    grads = grads.reshape(seq_count, part_rows, per_dev, width)
    dquery_rows = dquery.reshape(per_dev * DH, tokens)
    lower = dquery_rows[: DH // 2]
    upper = dquery_rows[DH // 2 :]
    outgoing = jnp.where(first, upper, lower)
    kept = jnp.where(first, lower, upper)
    incoming = from_partner(outgoing, "seq", 0)
    grad_query_t = (kept + incoming).astype(jnp.bfloat16)
    returned = lax.all_to_all(
        grads.reshape(seq_count, part_rows, per_dev * width),
        "seq",
        split_axis=0,
        concat_axis=0,
        tiled=True,
    )
    full_rows = to_rows(returned, blocks_h, split, part_rows, per_dev, width)
    half_cols = DH * blocks_h * per_dev
    key_part = full_rows[:, :half_cols]
    value_part = full_rows[:, half_cols:]
    key_sum, value_sum = (
        lax.psum_scatter(key_part, "grp", scatter_dimension=1, tiled=True),
        lax.psum_scatter(value_part, "grp", scatter_dimension=1, tiled=True),
    )
    grad_keys = key_sum.astype(jnp.bfloat16)
    grad_values = value_sum.astype(jnp.bfloat16)
    return (grad_query_t, grad_keys, grad_values)


def solution(mesh):
    placed = (
        P("seq", None),
        P("seq", "grp"),
        P("seq", "grp"),
        P(None, "grp"),
        P(None, "grp"),
        P("grp"),
    )
    return jax.shard_map(
        on_device,
        mesh=mesh,
        in_specs=placed,
        out_specs=(P("seq", "grp"), P("seq", "grp"), P("seq", "grp")),
        check_vma=False,
    )
```

profile of v0, /device:TPU:1, one launch (start us, length us, event | category | flops | bytes accessed | tf_op | source)
XLA Modules:
  0.0 228.4 jit_solution(502918772981266654)
XLA Ops:
  7.2 1.6 copy.17
  8.8 0.9 reshape.197
  9.7 2.9 %copy.18 = bf16[64,64,128]{2,1,0:T(8,128)(2,1)} copy(bf16[64,64,128]{1,0,2:T(8,128)(2,1)S(1)} %bitcast.98) | data formatting | bytes 2097152 | tf_op jit(solution)/shard_map/reshape | solution.py:33
  12.6 11.6 %all-to-all-start = ((bf16[64,64,128]{2,1,0:T(8,128)(2,1)}), bf16[64,64,128]{2,1,0:T(8,128)(2,1)S(1)}, u32[]{:S(2)}, u32[]{:S(2)}) async-start(bf16[64,64,128]{2,1,0:T(8,128)(2,1)} %copy.18), calls=%async_computation | async-start | bytes 2097152 | tf_op jit(solution)/shard_map/all_to_all | solution.py:34
  24.3 2.4 %collective-permute-start = (bf16[32,512]{1,0:T(8,128)(2,1)S(1)}, bf16[32,512]{1,0:T(8,128)(2,1)S(1)}, u32[]{:S(2)}, u32[]{:S(2)}) collective-permute-start(bf16[32,512]{1,0:T(8,128)(2,1)S(1)} %copy-done), channel_id=1, source_target_pairs={{0,1},{1,0},{2,3},{3,2},{4,5},{5,4},{6,7},{7,6},{8,9},{9,8},{10,11... | collective-permute-start | bytes 98312 | tf_op jit(solution)/shard_map/ppermute | solution.py:13
  26.7 2.0 collective-permute-start.1
  28.8 0.7 constant_dynamic-slice_fusion
  29.8 22.4 %all-to-all-done = bf16[64,64,128]{2,1,0:T(8,128)(2,1)S(1)} async-done(((bf16[64,64,128]{2,1,0:T(8,128)(2,1)}), bf16[64,64,128]{2,1,0:T(8,128)(2,1)S(1)}, u32[]{:S(2)}, u32[]{:S(2)}) %all-to-all-start) | async-done | bytes 1048608 | tf_op jit(solution)/shard_map/all_to_all | solution.py:34
  52.2 19.1 %while.13 = (s32[]{:T(128)}, f32[1,64,512]{2,1,0:T(8,128)S(1)}, f32[8,512,1,128]{3,1,0,2:T(8,128)}, bf16[8,512,1,128]{3,1,2,0:T(8,128)(2,1)S(1)}, pred[512]{0:T(...) while((s32[]{:T(128)}, f32[1,64,512]{2,1,0:T(8,128)S(1)}, ...), condition=%wide.region_2.3_spmd.clone, body=%wide.region_1.2_spmd.clone.sunk | while | flops 169738240 | bytes 7737991 | solution.py:81
  52.3 0.3 fusion.39
  52.9 0.3 fusion.40
  53.9 0.7 constant_dynamic-update-slice_fusion.2
  54.6 0.3 fusion.39
  54.9 0.3 convolution_bitcast_fusion.5
  55.2 0.3 fusion.40
  56.3 0.7 constant_dynamic-update-slice_fusion.2
  57.0 0.3 fusion.39
  57.6 0.3 fusion.40
  58.7 0.7 constant_dynamic-update-slice_fusion.2
  59.4 0.3 fusion.39
  60.0 0.3 fusion.40
  61.0 0.7 constant_dynamic-update-slice_fusion.2
  61.8 0.3 fusion.39
  62.4 0.3 fusion.40
  63.4 0.7 constant_dynamic-update-slice_fusion.2
  64.2 0.3 fusion.39
  64.8 0.3 fusion.40
  65.8 0.7 constant_dynamic-update-slice_fusion.2
  66.6 0.3 fusion.39
  67.2 0.3 fusion.40
  68.2 0.7 constant_dynamic-update-slice_fusion.2
  68.9 0.3 fusion.39
  69.6 0.3 fusion.40
  70.6 0.7 constant_dynamic-update-slice_fusion.2
  71.3 56.1 %all_to_all.10 = f32[64,64,128]{2,1,0:T(8,128)S(1)} all-to-all(f32[64,64,128]{2,1,0:T(8,128)} %bitcast.100), channel_id=1, replica_groups=mesh['grp'=8,'seq'=64] {'seq'}, dimensions={0} | all-to-all | bytes 4194304 | tf_op jit(solution)/shard_map/all_to_all | solution.py:90
  127.5 4.8 %copy.21 = f32[2,64,128,32,1]{1,0,3,2,4:T(2,128)} copy(f32[2,64,128,32,1]{2,1,0,3,4:T(8,128)S(1)} %bitcast.97) | data formatting | bytes 4194304 | tf_op jit(solution)/shard_map/transpose | solution.py:18
  132.3 4.3 %reshape.201 = f32[128,4096]{0,1:T(8,128)S(1)} reshape(f32[2,64,128,32,1]{1,0,3,2,4:T(2,128)} %copy.21) | data formatting | bytes 4194304 | tf_op jit(solution)/shard_map/reshape | solution.py:19
  136.6 1.5 fusion.19
  138.1 0.7 reduce-scatter.3.cloned.1.call-update
  138.8 4.0 %collective-permute-start.2 = (f32[32,512]{1,0:T(8,128)S(1)}, f32[32,512]{1,0:T(8,128)S(1)}, u32[]{:S(2)}, u32[]{:S(2)}) collective-permute-start(f32[32,512]{1,0:T(8,128)S(1)} %select_bitcast_fusion), channel_id=1, source_target_pairs={{0,1},{1,0},{2,3},{3,2},{4,5},{5,4},{6,7},{7,6},{8,9},{9,8},{10,11... | collective-permute-start | bytes 196616 | tf_op jit(solution)/shard_map/ppermute | solution.py:13
  142.9 0.9 collective-permute-done.2
  143.8 0.6 fusion.11
  144.4 32.3 %reduce-scatter.5.cloned.1.call-done = f32[128,256]{0,1:T(8,128)} async-done(((f32[128,2048]{0,1:T(8,128)}), f32[128,256]{0,1:T(8,128)}) %reduce-scatter.5.cloned.1.call-update) | async-done | bytes 131088 | tf_op jit(solution)/shard_map/reduce_scatter | solution.py:103
  176.7 0.9 convert_element_type.19
  177.6 0.7 copy.23
  178.3 41.6 %reduce-scatter.3.cloned.1.call-done = f32[128,256]{0,1:T(8,128)} async-done(((f32[128,2048]{0,1:T(8,128)}), f32[128,256]{0,1:T(8,128)}) %reduce-scatter.3.cloned.1.call-update) | async-done | bytes 131088 | tf_op jit(solution)/shard_map/reduce_scatter | solution.py:102
  219.9 0.9 convert_element_type.18
  220.8 0.7 copy.22
  (66 shorter events, 7.8 us)
Async XLA Ops:
  9.6 14.7 %copy-start = (bf16[32,512]{1,0:T(8,128)(2,1)S(1)}, bf16[32,512]{1,0:T(8,128)(2,1)}, u32[]{:S(2)}) copy-start(bf16[32,512]{1,0:T(8,128)(2,1)} %param.9) | copy-start | bytes 98308
  9.7 17.0 %copy-start.1 = (bf16[32,512]{1,0:T(8,128)(2,1)S(1)}, bf16[32,512]{1,0:T(8,128)(2,1)}, u32[]{:S(2)}) copy-start(bf16[32,512]{1,0:T(8,128)(2,1)} %param.10) | copy-start | bytes 98308
  9.7 19.0 %copy-start.2 = (s32[2]{0:T(128)S(1)}, s32[2]{0:T(128)}, u32[]{:S(2)}) copy-start(s32[2]{0:T(128)} %param.13) | copy-start | bytes 28
  12.6 39.6 %all-to-all-start = ((bf16[64,64,128]{2,1,0:T(8,128)(2,1)}), bf16[64,64,128]{2,1,0:T(8,128)(2,1)S(1)}, u32[]{:S(2)}, u32[]{:S(2)}) async-start(bf16[64,64,128]{2,1,0:T(8,128)(2,1)} %copy.18), calls=%async_computation | async-start | bytes 2097152 | tf_op jit(solution)/shard_map/all_to_all | solution.py:34
  24.3 152.4 %reduce-scatter.5.cloned.1.call-start = ((), (), s32[]{:S(2)}) async-start(), calls=%async_computation.5 | async-start | bytes 1179648 | tf_op jit(solution)/shard_map/reduce_scatter | solution.py:103
  24.3 5.2 %collective-permute-start = (bf16[32,512]{1,0:T(8,128)(2,1)S(1)}, bf16[32,512]{1,0:T(8,128)(2,1)S(1)}, u32[]{:S(2)}, u32[]{:S(2)}) collective-permute-start(bf16[32,512]{1,0:T(8,128)(2,1)S(1)} %copy-done), channel_id=1, source_target_pairs={{0,1},{1,0},{2,3},{3,2},{4,5},{5,4},{6,7},{7,6},{8,9},{9,8},{10,11... | collective-permute-start | bytes 98312 | tf_op jit(solution)/shard_map/ppermute | solution.py:13
  26.7 3.1 %collective-permute-start.1 = (bf16[32,512]{1,0:T(8,128)(2,1)S(1)}, bf16[32,512]{1,0:T(8,128)(2,1)S(1)}, u32[]{:S(2)}, u32[]{:S(2)}) collective-permute-start(bf16[32,512]{1,0:T(8,128)(2,1)S(1)} %copy-done.1), channel_id=1, source_target_pairs={{0,1},{1,0},{2,3},{3,2},{4,5},{5,4},{6,7},{7,6},{8,9},{9,8},{10,11... | collective-permute-start | bytes 98312 | tf_op jit(solution)/shard_map/ppermute | solution.py:13
  138.1 81.8 %reduce-scatter.3.cloned.1.call-start = ((), (), s32[]{:S(2)}) async-start(), calls=%async_computation.4 | async-start | bytes 1179648 | tf_op jit(solution)/shard_map/reduce_scatter | solution.py:102
  138.8 4.9 %collective-permute-start.2 = (f32[32,512]{1,0:T(8,128)S(1)}, f32[32,512]{1,0:T(8,128)S(1)}, u32[]{:S(2)}, u32[]{:S(2)}) collective-permute-start(f32[32,512]{1,0:T(8,128)S(1)} %select_bitcast_fusion), channel_id=1, source_target_pairs={{0,1},{1,0},{2,3},{3,2},{4,5},{5,4},{6,7},{7,6},{8,9},{9,8},{10,11... | collective-permute-start | bytes 196616 | tf_op jit(solution)/shard_map/ppermute | solution.py:13
Sparse Core Ops, SparseCore 0:
  138.2 38.4 reduce-scatter.4
  179.5 40.3 reduce-scatter.2
where the time goes:
time: 233 us; the launch traced here: 228 us
  waiting for transfers between devices  98.1 us (42%)
  blocking collectives  56.1 us (24%)
  local copies, waits for them, and re-layouts  25.1 us (11%)
  starting transfers between devices  20.1 us (9%)
  between operations  14.2 us (6%)
  matrix products  11.7 us (5%)
  other arithmetic  2.78 us (1%)
    all_to_all x1, blocking collectives, on_device(): lax.all_to_all(grads.reshape(seq_count, part_rows, per_dev * width), 'seq...  56.1 us
    reduce_scatter x1, waiting for transfers between devices, on_device(): lax.psum_scatter(key_part, 'grp', scatter_dimension=1, tiled=True)  41.6 us
    reduce_scatter x1, waiting for transfers between devices, on_device(): lax.psum_scatter(value_part, 'grp', scatter_dimension=1, tiled=True)  32.3 us
    all_to_all x1, waiting for transfers between devices, on_device(): lax.all_to_all(local, 'seq', split_axis=0, concat_axis=0, tiled=True)  22.4 us
    all_to_all x1, starting transfers between devices, on_device(): lax.all_to_all(local, 'seq', split_axis=0, concat_axis=0, tiled=True)  11.6 us
    ppermute x3, starting transfers between devices, from_partner(): lax.ppermute(shard, axis, [(i, i ^ 1 << stride) for i in range(lax.axis_s...  8.37 us
    dynamic_update_slice x16, local copies, waits for them, and re-layouts, on_device(): dquery, grads = lax.scan(step, start, pieces)  6.8 us
    transpose x1, local copies, waits for them, and re-layouts, to_rows(): shaped = jnp.transpose(shaped, (1, 2, 4, 0, 3))  4.82 us
  transfers between devices with their start and end apart: 6, of which 5 were waited for; matrix products, arithmetic and copies ran while one was open for 1% of the time, Pallas kernels for 0%

commit v1 on v0

v1 whole, which is shorter than its diff:
```python
import functools
import math

import jax
import jax.numpy as jnp
from jax import lax
from jax.experimental import pallas as pl
from jax.experimental.pallas import tpu as pltpu
from jax.sharding import PartitionSpec as P

DH = 64
LEN = 256
HALF = DH // 2
STATS = 16
PART = 2 * HALF + STATS
LANES = 128
MESH = pl.DeviceIdType.MESH
F32 = jnp.float32
BF16 = jnp.bfloat16

NT = (((1,), (1,)), ((), ()))
NN = (((1,), (0,)), ((), ()))


def dot(a, b, dims=NN):
    return lax.dot_general(a, b, dims, preferred_element_type=F32)


def exchange_lanes(tiles, unit):
    count = len(tiles)
    lane = lax.broadcasted_iota(jnp.int32, tiles[0].shape, 1)
    step = 1
    while step < count:
        shift = step * unit
        low = (lane & shift) == 0
        made = list(tiles)
        for a in range(count):
            if a & step == 0:
                x, y = tiles[a], tiles[a | step]
                made[a] = jnp.where(low, x, pltpu.roll(y, shift, 1))
                made[a | step] = jnp.where(low, pltpu.roll(x, LANES - shift, 1), y)
        tiles = made
        step *= 2
    return tiles


def kernel(
    n_z, n_h, keys_all,
    kv_hbm, q_hbm, g_hbm, ln_hbm, dl_hbm, len_ref,
    oq_ref, ok_ref, ov_ref,
    kvx, lnv, dlv, kvs, kvb, blocks, lhs, keys_t, acc,
    own_half, sent_half, got_half, dq_out, dq_in, z_out, z_in, p_out, p_in, wide,
    in_sem, kv_send, kv_recv, ring_send, ring_recv, pair_send, pair_recv,
    half_send, half_recv, dq_send, dq_recv, z_send, z_recv, p_send, p_recv,
):
    z = lax.axis_index("grp")
    s = lax.axis_index("seq")
    h = s // 2
    c = s - 2 * h
    partner = 2 * h + 1 - c
    kb = kvx.shape[0]
    tokens = blocks.shape[3]
    span = tokens // 2
    keys = n_h * kb
    last = n_z // 2
    dr = DH // n_z

    loads = [
        pltpu.make_async_copy(kv_hbm.at[pl.ds(pl.multiple_of(z * kb, kb), kb)], kvx, in_sem.at[0]),
        pltpu.make_async_copy(ln_hbm, lnv, in_sem.at[1]),
        pltpu.make_async_copy(dl_hbm, dlv, in_sem.at[2]),
        pltpu.make_async_copy(q_hbm, blocks.at[z, c, pl.ds(0, HALF)], in_sem.at[3]),
        pltpu.make_async_copy(g_hbm, blocks.at[z, c, pl.ds(HALF, HALF)], in_sem.at[4]),
    ]
    for load in loads:
        load.start()

    barrier = pltpu.get_barrier_semaphore()

    def greet_plane(i, _):
        to = lax.rem(h + i, n_h)
        pl.semaphore_signal(barrier, inc=1, device_id=(z, 2 * to + c), device_id_type=MESH)
        return 0

    def greet_line(i, _):
        pl.semaphore_signal(barrier, inc=1, device_id=(lax.rem(z + i, n_z), s), device_id_type=MESH)
        return 0

    lax.fori_loop(1, n_z, greet_line, 0)
    pl.semaphore_signal(barrier, inc=1, device_id=(z, partner), device_id_type=MESH)
    lax.fori_loop(1, n_h, greet_plane, 0)

    loads[1].wait()
    loads[2].wait()
    place = lax.broadcasted_iota(jnp.int32, (1, tokens), 1)
    limit = jnp.zeros((1, tokens), jnp.int32)
    for a in range(tokens // LEN):
        limit = jnp.where(place // LEN == a, len_ref[a], limit)
    norm = -(lnv[pl.ds(h, 1), :] + math.log(keys_all))
    norm = jnp.where(lax.rem(place, LEN) < limit, norm, -1e30)
    row = jnp.where(c == 0, norm, -dlv[pl.ds(h, 1), :])
    high = row.astype(BF16).astype(F32)
    middle = (row - high).astype(BF16).astype(F32)
    low = row - high - middle
    at = lax.broadcasted_iota(jnp.int32, (STATS, tokens), 0)
    rows = jnp.where(at == 0, high, jnp.where(at == 1, middle, jnp.where(at == 2, low, 0.0)))
    blocks[z, c, pl.ds(2 * HALF, STATS)] = rows.astype(BF16)
    loads[3].wait()
    loads[4].wait()

    loads[0].wait()
    tiles = [kvx[:, j * LANES : (j + 1) * LANES].astype(F32) for j in range(n_h)]
    tiles = exchange_lanes(tiles, 1)
    for j in range(n_h):
        kvs[j] = tiles[j].astype(BF16)
    kvb[pl.ds(h, 1)] = kvs[pl.ds(h, 1)]

    pl.semaphore_wait(barrier, n_h - 1 + n_z)

    def ring(way, t, block, columns):
        to = lax.rem(z + (1 if way == 0 else n_z - 1), n_z)
        ref = blocks.at[block, c, :, columns]
        return pltpu.make_async_remote_copy(
            src_ref=ref, dst_ref=ref,
            send_sem=ring_send.at[way, t], recv_sem=ring_recv.at[way, t],
            device_id=(to, s), device_id_type=MESH,
        )

    def pair(i, block):
        ref = blocks.at[block, c]
        return pltpu.make_async_remote_copy(
            src_ref=ref, dst_ref=ref,
            send_sem=pair_send.at[i], recv_sem=pair_recv.at[i],
            device_id=(z, partner), device_id_type=MESH,
        )

    every = pl.ds(0, tokens)
    halves = (pl.ds(0, span), pl.ds(span, span))

    def order(i):
        t = (i + 1) // 2
        return lax.rem(jnp.where(lax.rem(i, 2) == 1, z - t, z + t) + n_z, n_z)

    for way in (0, 1):
        ring(way, 1, z, every if last > 1 else halves[way]).start()
    pair(0, z).start()

    def send_kv(i, _):
        to = lax.rem(h + i, n_h)
        pltpu.make_async_remote_copy(
            src_ref=kvs.at[to], dst_ref=kvb.at[h], send_sem=kv_send, recv_sem=kv_recv,
            device_id=(z, 2 * to + c), device_id_type=MESH,
        ).start()
        return 0

    lax.fori_loop(1, n_h, send_kv, 0)

    def arrive(t):
        @pl.when(t < last)
        def _():
            for way in (0, 1):
                block = order(2 * t - 1 + way)
                ring(way, t, block, every).wait_recv()

                @pl.when(t + 1 < last)
                def _():
                    ring(way, t + 1, block, every).start()

                @pl.when(t + 1 == last)
                def _():
                    ring(way, t + 1, block, halves[way]).start()

                pair(2 * t - 1 + way, block).start()

        @pl.when(t == last)
        def _():
            block = order(n_z - 1)
            for way in (0, 1):
                ring(way, last, block, halves[way]).wait_recv()
            pair(n_z - 1, block).start()

    arrive(jnp.int32(1))

    lane = lax.broadcasted_iota(jnp.int32, (LANES, 2 * PART), 0)
    channel = lax.rem(lane, n_h) * (LANES // n_h) + lane // n_h
    col = lax.broadcasted_iota(jnp.int32, (LANES, 2 * PART), 1)
    side = col // PART
    within = col - side * PART
    is_key = within < HALF
    is_value = (within >= HALF) & (within < 2 * HALF)
    for_scores = jnp.where(is_key & (channel == side * HALF + within), 1.0, 0.0).astype(BF16)
    for_dprobs = jnp.where(
        is_value & (channel == DH + side * HALF + within - HALF), 1.0, 0.0
    ).astype(BF16)
    one = lax.broadcasted_iota(jnp.int32, (keys, 2 * PART), 1)
    ones_s = jnp.where((one >= 2 * HALF) & (one < 2 * HALF + 3), 1.0, 0.0)
    ones_p = jnp.where((one >= PART + 2 * HALF) & (one < PART + 2 * HALF + 3), 1.0, 0.0)
    lane_t = lax.broadcasted_iota(jnp.int32, (DH, LANES), 1)
    channel_t = lax.rem(lane_t, n_h) * (LANES // n_h) + lane_t // n_h
    row_t = lax.broadcasted_iota(jnp.int32, (DH, LANES), 0)
    for_keys = jnp.where(channel_t == row_t, 1.0, 0.0).astype(BF16)

    pltpu.make_async_copy(kvb.at[pl.ds(0, n_h - 1)], kvb.at[pl.ds(0, n_h - 1)], kv_recv).wait()
    mixed = kvb[...].reshape(keys, LANES)
    lhs[0] = (dot(mixed, for_scores) + ones_s).astype(BF16)
    lhs[1] = (dot(mixed, for_dprobs) + ones_p).astype(BF16)
    keys_t[...] = dot(for_keys, mixed, NT).astype(BF16)
    acc[...] = jnp.zeros_like(acc)

    def swap_half(i):
        return pltpu.make_async_remote_copy(
            src_ref=sent_half.at[i], dst_ref=got_half.at[i],
            send_sem=half_send.at[i], recv_sem=half_recv.at[i],
            device_id=(z, partner), device_id_type=MESH,
        )

    def dq_copy(i):
        return pltpu.make_async_remote_copy(
            src_ref=dq_out.at[i], dst_ref=dq_in.at[i], send_sem=dq_send, recv_sem=dq_recv,
            device_id=(order(i), s), device_id_type=MESH,
        )

    def combine(i):
        swap_half(i).wait_recv()
        total = own_half[i] + got_half[i]
        own_half[i] = total
        dq_out[i] = total.astype(BF16)

        @pl.when(i > 0)
        def _():
            dq_copy(i).start()

    chunk = min(keys, 256)

    def compute(i, _):
        @pl.when((lax.rem(i, 2) == 1) & (i // 2 + 2 <= last))
        def _():
            arrive(i // 2 + 2)

        block = order(i)
        pltpu.make_async_copy(
            blocks.at[block, 1 - c], blocks.at[block, 1 - c], pair_recv.at[i]
        ).wait()
        rhs = blocks[block].reshape(2 * PART, tokens)
        blank = jnp.zeros((DH, tokens), BF16)
        q_rows = jnp.concatenate([rhs[:HALF], rhs[PART : PART + HALF], blank], 0)
        g_rows = jnp.concatenate([blank, rhs[HALF:DH], rhs[PART + HALF : PART + DH]], 0)
        dq = jnp.zeros((DH, tokens), F32)
        for k in range(0, keys, chunk):
            part = slice(k, k + chunk)
            probs = jnp.exp(dot(lhs[0, part], rhs))
            dscores = probs * dot(lhs[1, part], rhs)
            probs = probs.astype(BF16)
            dscores = dscores.astype(BF16)
            acc[part] += dot(dscores, q_rows, NT) + dot(probs, g_rows, NT)
            dq += dot(keys_t[:, part], dscores)
        top, bottom = dq[:HALF], dq[HALF:]
        own_half[i] = jnp.where(c == 0, top, bottom)
        sent_half[i] = jnp.where(c == 0, bottom, top)
        swap_half(i).start()

        @pl.when(i > 0)
        def _():
            combine(i - 1)

        return 0

    lax.fori_loop(0, n_z, compute, 0)

    turned = acc[...].T.reshape(2, n_z, dr, keys)
    for g in range(n_z):
        z_out[g] = jnp.concatenate([turned[0, g], turned[1, g]], 0).astype(BF16)
    z_in[pl.ds(z, 1)] = z_out[pl.ds(z, 1)]

    def send_z(i, _):
        to = lax.rem(z + i, n_z)
        pltpu.make_async_remote_copy(
            src_ref=z_out.at[to], dst_ref=z_in.at[z], send_sem=z_send, recv_sem=z_recv,
            device_id=(to, s), device_id_type=MESH,
        ).start()
        return 0

    lax.fori_loop(1, n_z, send_z, 0)
    combine(n_z - 1)
    pltpu.make_async_copy(z_in.at[pl.ds(0, n_z - 1)], z_in.at[pl.ds(0, n_z - 1)], z_recv).wait()

    for j in range(keys // LANES):
        tiles = [z_in[a, :, j * LANES : (j + 1) * LANES].astype(F32) for a in range(n_z)]
        tiles = exchange_lanes(tiles, kb)
        for a in range(n_z):
            p_out[j * n_z + a] = tiles[a].astype(BF16)
    p_in[pl.ds(h, 1)] = p_out[pl.ds(h, 1)]

    def send_p(i, _):
        to = lax.rem(h + i, n_h)
        pltpu.make_async_remote_copy(
            src_ref=p_out.at[to], dst_ref=p_in.at[h], send_sem=p_send, recv_sem=p_recv,
            device_id=(z, 2 * to + c), device_id_type=MESH,
        ).start()
        return 0

    lax.fori_loop(1, n_h, send_p, 0)

    pltpu.make_async_copy(dq_in.at[pl.ds(1, n_z - 1)], dq_in.at[pl.ds(1, n_z - 1)], dq_recv).wait()
    total = own_half[0]
    for i in range(1, n_z):
        total = total + dq_in[i].astype(F32)
    oq_ref[...] = total.astype(BF16)

    pltpu.make_async_copy(p_in.at[pl.ds(0, n_h - 1)], p_in.at[pl.ds(0, n_h - 1)], p_recv).wait()
    wide[...] = p_in[...].astype(F32).reshape(n_h * 2 * dr, LANES)
    for which, ref in enumerate((ok_ref, ov_ref)):
        rows = [wide[pl.ds(which * dr + d, n_h, stride=2 * dr), :] for d in range(dr)]
        ref[...] = jnp.concatenate(rows, 0).T.astype(BF16)

    for way in (0, 1):
        for t in range(1, last + 1):
            ring(way, t, z, every if t < last else halves[way]).wait_send()
    for i in range(n_z):
        pair(i, z).wait_send()
        swap_half(i).wait_send()
    for buf, n, sem in (
        (kvs, n_h - 1, kv_send),
        (dq_out, n_z - 1, dq_send),
        (z_out, n_z - 1, z_send),
        (p_out, n_h - 1, p_send),
    ):
        pltpu.make_async_copy(buf.at[pl.ds(0, n)], buf.at[pl.ds(0, n)], sem).wait()


def on_device(kv_states, queries_t, grad_out_t, log_norm, delta, lengths):
    n_z, n_s = lax.axis_size("grp"), lax.axis_size("seq")
    n_h = n_s // 2
    rows, cols = kv_states.shape
    tokens = queries_t.shape[1]
    kb = rows // n_z
    keys = n_h * kb
    dr = DH // n_z
    last = n_z // 2
    hbm = pl.BlockSpec(memory_space=pl.ANY)
    vmem = pl.BlockSpec(memory_space=pltpu.VMEM)
    dma = pltpu.SemaphoreType.DMA
    return pl.pallas_call(
        functools.partial(kernel, n_z, n_h, rows * n_s),
        out_shape=(
            jax.ShapeDtypeStruct((HALF, tokens), BF16),
            jax.ShapeDtypeStruct((rows, dr * n_h), BF16),
            jax.ShapeDtypeStruct((rows, dr * n_h), BF16),
        ),
        in_specs=[hbm] * 5 + [pl.BlockSpec(memory_space=pltpu.SMEM)],
        out_specs=(vmem,) * 3,
        scratch_shapes=[
            pltpu.VMEM((kb, cols), BF16),
            pltpu.VMEM((n_h, tokens), F32),
            pltpu.VMEM((n_h, tokens), F32),
            pltpu.VMEM((n_h, kb, LANES), BF16),
            pltpu.VMEM((n_h, kb, LANES), BF16),
            pltpu.VMEM((n_z, 2, PART, tokens), BF16),
            pltpu.VMEM((2, keys, 2 * PART), BF16),
            pltpu.VMEM((DH, keys), BF16),
            pltpu.VMEM((keys, 2 * DH), F32),
            pltpu.VMEM((n_z, HALF, tokens), F32),
            pltpu.VMEM((n_z, HALF, tokens), F32),
            pltpu.VMEM((n_z, HALF, tokens), F32),
            pltpu.VMEM((n_z, HALF, tokens), BF16),
            pltpu.VMEM((n_z, HALF, tokens), BF16),
            pltpu.VMEM((n_z, 2 * dr, keys), BF16),
            pltpu.VMEM((n_z, 2 * dr, keys), BF16),
            pltpu.VMEM((n_h, 2 * dr, LANES), BF16),
            pltpu.VMEM((n_h, 2 * dr, LANES), BF16),
            pltpu.VMEM((n_h * 2 * dr, LANES), F32),
            dma((5,)),
            dma, dma,
            dma((2, last + 1)), dma((2, last + 1)),
            dma((n_z,)), dma((n_z,)),
            dma((n_z,)), dma((n_z,)),
            dma, dma, dma, dma, dma, dma,
        ],
        compiler_params=pltpu.CompilerParams(
            collective_id=0, has_side_effects=True, vmem_limit_bytes=48 * 1024 * 1024
        ),
        cost_estimate=pl.CostEstimate(
            flops=10 * DH * keys * tokens * n_z,
            bytes_accessed=4 * 1024 * 1024,
            transcendentals=keys * tokens * n_z,
        ),
    )(kv_states, queries_t, grad_out_t, log_norm, delta, lengths)


def solution(mesh):
    placed = (
        P("seq", None),
        P("seq", "grp"),
        P("seq", "grp"),
        P(None, "grp"),
        P(None, "grp"),
        P("grp"),
    )
    return jax.shard_map(
        on_device,
        mesh=mesh,
        in_specs=placed,
        out_specs=(P("seq", "grp"), P("seq", "grp"), P("seq", "grp")),
        check_vma=False,
    )
```

time: 233 us -> 58.5 us (0.25); the launches traced: 228 us -> 58.1 us
  waiting for transfers between devices: 98.1 us -> 0 us
  blocking collectives: 56.1 us -> 0 us
  Pallas kernels: 0 us -> 50.5 us
  starting transfers between devices: 20.1 us -> 0 us
  local copies, waits for them, and re-layouts: 25.1 us -> 6.94 us
  between operations: 14.2 us -> 0.65 us
  matrix products: 11.7 us -> 0 us
  other arithmetic: 2.78 us -> 0 us
    reduce_scatter x2 -> x0, waiting for transfers between devices: 73.8 us -> none  [the longest x1 41.6 us: on_device(): lax.psum_scatter(key_part, 'grp', scatter_dimension=1, tiled=True)]
    all_to_all x1 -> x0, blocking collectives: 56.1 us -> none  [on_device(): lax.all_to_all(grads.reshape(seq_count, part_rows, per_dev * width), 'seq...]
    pallas_call x0 -> x1, Pallas kernels: none -> 50.5 us  [on_device(): pl.pallas_call(functools.partial(kernel, n_z, n_h, rows * n_s), out_shape...]
    all_to_all x1 -> x0, waiting for transfers between devices: 22.4 us -> none  [on_device(): lax.all_to_all(local, 'seq', split_axis=0, concat_axis=0, tiled=True)]
    dot_general x40 -> x0, matrix products: 11.7 us -> none  [the longest x8 2.76 us: step(): jnp.einsum('hdt,khd->htk', g_heads, vals_b, preferred_element_type=jnp.fl...]
    all_to_all x1 -> x0, starting transfers between devices: 11.6 us -> none  [on_device(): lax.all_to_all(local, 'seq', split_axis=0, concat_axis=0, tiled=True)]
    ppermute x3 -> x0, starting transfers between devices: 8.37 us -> none  [from_partner(): lax.ppermute(shard, axis, [(i, i ^ 1 << stride) for i in range(lax.axis_s...]
    reshape x3 -> x0, local copies, waits for them, and re-layouts: 8.08 us -> none  [the longest x1 4.29 us: to_rows(): return shaped.reshape(split * part_rows, cols * blocks_h * per_dev)]
  transfers between devices with their start and end apart: 6 -> 0, of which waited for: 5 -> 0; matrix products, arithmetic and copies ran while one was open for 1% -> 0% of each run, Pallas kernels for 0% -> 0%
where the time goes in v1:
time: 58.5 us; the launch traced here: 58.1 us
  Pallas kernels  50.5 us (86%)
  local copies, waits for them, and re-layouts  6.94 us (12%)
  between operations  0.65 us (1%)
    pallas_call x1, Pallas kernels, on_device(): pl.pallas_call(functools.partial(kernel, n_z, n_h, rows * n_s), out_shape...  50.5 us
    unnamed x15, local copies, waits for them, and re-layouts  6.94 us

profile of v1, /device:TPU:1, one launch (start us, length us, event | category | flops | bytes accessed | tf_op | source)
XLA Modules:
  0.0 58.1 jit_solution(14455403741924234065)
XLA Ops:
  0.6 0.0 copy-start
  0.6 1.2 %copy-done = bf16[128,4096]{1,0:T(8,128)(2,1)S(1)} copy-done((bf16[128,4096]{1,0:T(8,128)(2,1)S(1)}, bf16[128,4096]{1,0:T(8,128)(2,1)}, u32[]{:S(2)}) %copy-start) | copy-done | bytes 1048600
  1.9 0.0 copy-start.1
  1.9 0.8 %copy-done.1 = f32[32,512]{1,0:T(8,128)S(1)} copy-done((f32[32,512]{1,0:T(8,128)S(1)}, f32[32,512]{1,0:T(8,128)}, u32[]{:S(2)}) %copy-start.1) | copy-done | bytes 65560
  2.7 0.0 copy-start.2
  2.7 0.8 %copy-done.2 = f32[32,512]{1,0:T(8,128)S(1)} copy-done((f32[32,512]{1,0:T(8,128)S(1)}, f32[32,512]{1,0:T(8,128)}, u32[]{:S(2)}) %copy-start.2) | copy-done | bytes 65560
  3.5 0.0 copy-start.3
  3.5 0.8 %copy-done.3 = bf16[32,512]{1,0:T(8,128)(2,1)S(1)} copy-done((bf16[32,512]{1,0:T(8,128)(2,1)S(1)}, bf16[32,512]{1,0:T(8,128)(2,1)}, u32[]{:S(2)}) %copy-start.3) | copy-done | bytes 32792
  4.3 0.0 copy-start.4
  4.3 0.8 %copy-done.4 = bf16[32,512]{1,0:T(8,128)(2,1)S(1)} copy-done((bf16[32,512]{1,0:T(8,128)(2,1)S(1)}, bf16[32,512]{1,0:T(8,128)(2,1)}, u32[]{:S(2)}) %copy-start.4) | copy-done | bytes 32792
  5.1 0.0 copy-start.5
  5.1 0.7 %copy-done.5 = s32[2]{0:T(128)S(1)} copy-done((s32[2]{0:T(128)S(1)}, s32[2]{0:T(128)}, u32[]{:S(2)}) %copy-start.5) | copy-done | bytes 32
  5.7 50.5 %shard_map.85 = (bf16[32,512]{1,0:T(8,128)(2,1)S(1)}, bf16[128,256]{1,0:T(8,128)(2,1)S(1)}, bf16[128,256]{1,0:T(8,128)(2,1)S(1)}) custom-call(bf16[128,4096]{1,0:T(8,128)(2,1)S(1)} %copy-done, bf16[32,512]{1,0:T(8,128)(2,1)S(1)} %copy-done.3, bf16[32,512]{1,0:T(8,128)(2,1)S(1)} %copy-done.4, f32[32,512]{1,0:T(8,128)S(1)} %copy-done.1, ...), custom_call_target="tpu_custom_call" | custom-call | flops 1342177280 | bytes 4194304 | tf_op jit(solution)/shard_map/pallas_call | solution.py:343
  56.2 0.6 %copy.12 = bf16[32,512]{1,0:T(8,128)(2,1)} copy(bf16[32,512]{1,0:T(8,128)(2,1)S(1)} %get-tuple-element.6) | data formatting | bytes 65536
  56.8 0.6 %copy.13 = bf16[128,256]{1,0:T(8,128)(2,1)} copy(bf16[128,256]{1,0:T(8,128)(2,1)S(1)} %get-tuple-element.7) | data formatting | bytes 131072
  57.5 0.6 %copy.14 = bf16[128,256]{1,0:T(8,128)(2,1)} copy(bf16[128,256]{1,0:T(8,128)(2,1)S(1)} %get-tuple-element.8) | data formatting | bytes 131072
Async XLA Ops:
  0.6 1.2 %copy-start = (bf16[128,4096]{1,0:T(8,128)(2,1)S(1)}, bf16[128,4096]{1,0:T(8,128)(2,1)}, u32[]{:S(2)}) copy-start(bf16[128,4096]{1,0:T(8,128)(2,1)} %kv_hbm.1) | copy-start | bytes 3145732
  1.9 0.8 %copy-start.1 = (f32[32,512]{1,0:T(8,128)S(1)}, f32[32,512]{1,0:T(8,128)}, u32[]{:S(2)}) copy-start(f32[32,512]{1,0:T(8,128)} %ln_hbm.1) | copy-start | bytes 196612
  2.7 0.8 %copy-start.2 = (f32[32,512]{1,0:T(8,128)S(1)}, f32[32,512]{1,0:T(8,128)}, u32[]{:S(2)}) copy-start(f32[32,512]{1,0:T(8,128)} %dl_hbm.1) | copy-start | bytes 196612
  3.5 0.8 %copy-start.3 = (bf16[32,512]{1,0:T(8,128)(2,1)S(1)}, bf16[32,512]{1,0:T(8,128)(2,1)}, u32[]{:S(2)}) copy-start(bf16[32,512]{1,0:T(8,128)(2,1)} %q_hbm.1) | copy-start | bytes 98308
  4.3 0.8 %copy-start.4 = (bf16[32,512]{1,0:T(8,128)(2,1)S(1)}, bf16[32,512]{1,0:T(8,128)(2,1)}, u32[]{:S(2)}) copy-start(bf16[32,512]{1,0:T(8,128)(2,1)} %g_hbm.1) | copy-start | bytes 98308
  5.1 0.7 %copy-start.5 = (s32[2]{0:T(128)S(1)}, s32[2]{0:T(128)}, u32[]{:S(2)}) copy-start(s32[2]{0:T(128)} %len_ref.1) | copy-start | bytes 28

commit v2 on v1

v2 whole, which is shorter than its diff:
```python
import functools
import math

import jax
import jax.numpy as jnp
from jax import lax
from jax.experimental import pallas as pl
from jax.experimental.pallas import tpu as pltpu
from jax.sharding import PartitionSpec as P

DH = 64
LEN = 256
HALF = DH // 2
STATS = 16
PART = 2 * HALF + STATS
LANES = 128
MESH = pl.DeviceIdType.MESH
F32 = jnp.float32
BF16 = jnp.bfloat16

NT = (((1,), (1,)), ((), ()))
NN = (((1,), (0,)), ((), ()))


def dot(a, b, dims=NN):
    return lax.dot_general(a, b, dims, preferred_element_type=F32)


def exchange_lanes(tiles, unit):
    count = len(tiles)
    lane = lax.broadcasted_iota(jnp.int32, tiles[0].shape, 1)
    step = 1
    while step < count:
        shift = step * unit
        low = (lane & shift) == 0
        made = list(tiles)
        for a in range(count):
            if a & step == 0:
                x, y = tiles[a], tiles[a | step]
                made[a] = jnp.where(low, x, pltpu.roll(y, shift, 1))
                made[a | step] = jnp.where(low, pltpu.roll(x, LANES - shift, 1), y)
        tiles = made
        step *= 2
    return tiles


def kernel(
    n_z, n_h, keys_all,
    kv_hbm, q_hbm, g_hbm, ln_hbm, dl_hbm, len_ref,
    oq_ref, ok_ref, ov_ref,
    kvx, lnv, dlv, kvs, kvb, blocks, lhs, keys_t, acc,
    own_half, sent_half, got_half, dq_out, dq_in, p_out, p_in, wide,
    in_sem, kv_send, kv_recv, near_send, near_recv, far_send, far_recv,
    third_send, third_recv, fourth_send, fourth_recv, pair_send, pair_recv,
    half_send, half_recv, dq_send, dq_recv, p_send, p_recv,
):
    z = lax.axis_index("grp")
    s = lax.axis_index("seq")
    h = s // 2
    c = s - 2 * h
    partner = 2 * h + 1 - c
    rows = kvx.shape[0]
    tokens = blocks.shape[3]
    span = tokens // 2
    slots = kvb.shape[0]
    keys = slots * rows
    dr = DH // n_z

    width = n_z // 2
    run = h // width
    is_source = (lax.rem(h - run + n_h * width, width) == z // 2) & (c == lax.rem(z, 2))
    serves = lax.rem(run, 2)

    def source(slot):
        at = 2 * slot + c
        return 2 * (at * width + lax.rem(z // 2 + at, width)) + lax.rem(z, 2)

    own_slot = run // 2
    to_self = is_source & (serves == c)

    barrier = pltpu.get_barrier_semaphore()

    def greet(device):
        pl.semaphore_signal(barrier, inc=1, device_id=device, device_id_type=MESH)

    def greet_source(i, _):
        @pl.when(source(i) != s)
        def _():
            greet((z, source(i)))

        return 0

    def greet_line(i, _):
        greet((lax.rem(z + i, n_z), s))
        return 0

    lax.fori_loop(0, slots, greet_source, 0)
    lax.fori_loop(1, n_z, greet_line, 0)
    greet((z, partner))

    loads = [
        pltpu.make_async_copy(ln_hbm, lnv, in_sem.at[0]),
        pltpu.make_async_copy(dl_hbm, dlv, in_sem.at[1]),
        pltpu.make_async_copy(q_hbm, blocks.at[z, c, pl.ds(0, HALF)], in_sem.at[2]),
        pltpu.make_async_copy(g_hbm, blocks.at[z, c, pl.ds(HALF, HALF)], in_sem.at[3]),
    ]
    for load in loads:
        load.start()
    load_kv = pltpu.make_async_copy(kv_hbm, kvx, in_sem.at[4])

    @pl.when(is_source)
    def _():
        load_kv.start()

    loads[0].wait()
    loads[1].wait()
    place = lax.broadcasted_iota(jnp.int32, (1, tokens), 1)
    limit = jnp.zeros((1, tokens), jnp.int32)
    for a in range(tokens // LEN):
        limit = jnp.where(place // LEN == a, len_ref[a], limit)
    norm = -(lnv[pl.ds(h, 1), :] + math.log(keys_all))
    norm = jnp.where(lax.rem(place, LEN) < limit, norm, -1e30)
    row = jnp.where(c == 0, norm, -dlv[pl.ds(h, 1), :])
    high = row.astype(BF16).astype(F32)
    middle = (row - high).astype(BF16).astype(F32)
    low = row - high - middle
    at = lax.broadcasted_iota(jnp.int32, (STATS, tokens), 0)
    parts = jnp.where(at == 0, high, jnp.where(at == 1, middle, jnp.where(at == 2, low, 0.0)))
    blocks[z, c, pl.ds(2 * HALF, STATS)] = parts.astype(BF16)
    loads[2].wait()
    loads[3].wait()

    @pl.when(is_source)
    def _():
        load_kv.wait()

        def sort(r, _):
            part = pl.ds(pl.multiple_of(r * STATS, STATS), STATS)
            tiles = [kvx[part, j * LANES : (j + 1) * LANES].astype(F32) for j in range(n_h)]
            tiles = exchange_lanes(tiles, 1)
            for j in range(n_h):
                kvs[j, part] = tiles[j].astype(BF16)
            return 0

        lax.fori_loop(0, rows // STATS, sort, 0)

        @pl.when(serves == c)
        def _():
            kvb[pl.ds(own_slot, 1)] = kvs[pl.ds(h, 1)]

    served = jnp.where(is_source, n_h - jnp.where(serves == c, 1, 0), 0)
    pl.semaphore_wait(barrier, n_z + served)

    every = pl.ds(0, tokens)
    halves = (pl.ds(0, span), pl.ds(span, span))

    def order(i):
        t = (i + 1) // 2
        return lax.rem(jnp.where(lax.rem(i, 2) == 1, z - t, z + t) + n_z, n_z)

    def along(way, hops, block, columns, send, recv):
        to = lax.rem(z + (hops if way == 0 else n_z - hops), n_z)
        ref = blocks.at[block, c, :, columns]
        return pltpu.make_async_remote_copy(
            src_ref=ref, dst_ref=ref, send_sem=send, recv_sem=recv,
            device_id=(to, s), device_id_type=MESH,
        )

    def near(way):
        return along(way, 1, z, every, near_send.at[way], near_recv.at[way])

    def far(way, half):
        return along(way, 2, z, halves[half], far_send.at[way, half], far_recv.at[way, half])

    def third(way, half):
        block = order(3 + way)
        return along(way, 1, block, halves[half], third_send.at[way, half], third_recv.at[way, half])

    def fourth(way):
        return along(way, 2, order(3 + way), halves[way], fourth_send.at[way], fourth_recv.at[way])

    def pair(i):
        ref = blocks.at[order(i), c]
        return pltpu.make_async_remote_copy(
            src_ref=ref, dst_ref=ref,
            send_sem=pair_send.at[i], recv_sem=pair_recv.at[i],
            device_id=(z, partner), device_id_type=MESH,
        )

    for half in (0, 1):
        for way in (0, 1):
            far(way, half).start()
    for way in (0, 1):
        near(way).start()
    pair(0).start()

    def kv_copy(to):
        return pltpu.make_async_remote_copy(
            src_ref=kvs.at[to], dst_ref=kvb.at[own_slot],
            send_sem=kv_send, recv_sem=kv_recv.at[own_slot],
            device_id=(z, 2 * to + serves), device_id_type=MESH,
        )

    def send_kv(i, _):
        to = lax.rem(h + n_h // 2 + i, n_h)

        @pl.when(2 * to + serves != s)
        def _():
            kv_copy(to).start()

        return 0

    @pl.when(is_source)
    def _():
        lax.fori_loop(0, n_h, send_kv, 0)

    lane = lax.broadcasted_iota(jnp.int32, (LANES, 2 * PART), 0)
    channel = lax.rem(lane, n_h) * (LANES // n_h) + lane // n_h
    col = lax.broadcasted_iota(jnp.int32, (LANES, 2 * PART), 1)
    side = col // PART
    within = col - side * PART
    is_key = within < HALF
    is_value = (within >= HALF) & (within < 2 * HALF)
    for_scores = jnp.where(is_key & (channel == side * HALF + within), 1.0, 0.0).astype(BF16)
    for_dprobs = jnp.where(
        is_value & (channel == DH + side * HALF + within - HALF), 1.0, 0.0
    ).astype(BF16)
    one = lax.broadcasted_iota(jnp.int32, (1, 2 * PART), 1)
    ones_s = jnp.where((one >= 2 * HALF) & (one < 2 * HALF + 3), 1.0, 0.0)
    ones_p = jnp.where((one >= PART + 2 * HALF) & (one < PART + 2 * HALF + 3), 1.0, 0.0)
    lane_t = lax.broadcasted_iota(jnp.int32, (DH, LANES), 1)
    channel_t = lax.rem(lane_t, n_h) * (LANES // n_h) + lane_t // n_h
    row_t = lax.broadcasted_iota(jnp.int32, (DH, LANES), 0)
    for_keys = jnp.where(channel_t == row_t, 1.0, 0.0).astype(BF16)
    acc[...] = jnp.zeros_like(acc)

    for half in (0, 1):
        for way in (0, 1):
            far(way, half).wait_recv()
            third(way, half).start()
            if way == half:
                fourth(way).start()
    for way in (0, 1):
        near(way).wait_recv()
        pair(1 + way).start()
    for way in (0, 1):
        pair(3 + way).start()

    for slot in range(slots):

        @pl.when(jnp.logical_not(to_self & (own_slot == slot)))
        def _():
            pltpu.make_async_copy(kvb.at[slot], kvb.at[slot], kv_recv.at[slot]).wait()

    mixed = kvb[...].reshape(keys, LANES)
    lhs[0] = (dot(mixed, for_scores) + ones_s).astype(BF16)
    lhs[1] = (dot(mixed, for_dprobs) + ones_p).astype(BF16)
    keys_t[...] = dot(for_keys, mixed, NT).astype(BF16)

    def swap_half(i):
        return pltpu.make_async_remote_copy(
            src_ref=sent_half.at[i], dst_ref=got_half.at[i],
            send_sem=half_send.at[i], recv_sem=half_recv.at[i],
            device_id=(z, partner), device_id_type=MESH,
        )

    def dq_copy(i):
        return pltpu.make_async_remote_copy(
            src_ref=dq_out.at[i], dst_ref=dq_in.at[i], send_sem=dq_send, recv_sem=dq_recv,
            device_id=(order(i), s), device_id_type=MESH,
        )

    def combine(i):
        swap_half(i).wait_recv()
        total = own_half[i] + got_half[i]
        own_half[i] = total
        dq_out[i] = total.astype(BF16)

        @pl.when(i > 0)
        def _():
            dq_copy(i).start()

    chunk = min(keys, 256)

    def compute(i, _):
        @pl.when(i == 3)
        def _():
            for way in (0, 1):
                for half in (0, 1):
                    third(way, half).wait_recv()
                pair(5 + way).start()

        @pl.when(i == 5)
        def _():
            for way in (0, 1):
                fourth(way).wait_recv()
            pair(7).start()

        block = order(i)
        pltpu.make_async_copy(
            blocks.at[block, 1 - c], blocks.at[block, 1 - c], pair_recv.at[i]
        ).wait()
        rhs = blocks[block].reshape(2 * PART, tokens)
        blank = jnp.zeros((DH, tokens), BF16)
        q_rows = jnp.concatenate([rhs[:HALF], rhs[PART : PART + HALF], blank], 0)
        g_rows = jnp.concatenate([blank, rhs[HALF:DH], rhs[PART + HALF : PART + DH]], 0)
        dq = jnp.zeros((DH, tokens), F32)
        for k in range(0, keys, chunk):
            part = slice(k, k + chunk)
            probs = jnp.exp(dot(lhs[0, part], rhs))
            dscores = probs * dot(lhs[1, part], rhs)
            probs = probs.astype(BF16)
            dscores = dscores.astype(BF16)
            acc[part] += dot(dscores, q_rows, NT) + dot(probs, g_rows, NT)
            dq += dot(keys_t[:, part], dscores)
        top, bottom = dq[:HALF], dq[HALF:]
        own_half[i] = jnp.where(c == 0, top, bottom)
        sent_half[i] = jnp.where(c == 0, bottom, top)
        swap_half(i).start()

        @pl.when(i > 0)
        def _():
            combine(i - 1)

        return 0

    lax.fori_loop(0, n_z, compute, 0)

    turned = acc[...].T.reshape(2, n_z, dr, keys)
    for slot in range(slots):
        columns = slice(slot * rows, (slot + 1) * rows)
        for g in range(n_z):
            tile = jnp.concatenate([turned[0, g, :, columns], turned[1, g, :, columns]], 0)
            p_out[slot * n_z + g] = tile.astype(BF16)

    @pl.when(to_self)
    def _():
        p_in[pl.ds(h, 1)] = p_out[pl.ds(own_slot * n_z + z, 1)]

    def send_p(i, _):
        slot = lax.rem(i // n_z + h, slots)
        g = lax.rem(z + n_z // 2 + i, n_z)

        @pl.when((g != z) | (source(slot) != s))
        def _():
            pltpu.make_async_remote_copy(
                src_ref=p_out.at[slot * n_z + g], dst_ref=p_in.at[h],
                send_sem=p_send, recv_sem=p_recv,
                device_id=(g, source(slot)), device_id_type=MESH,
            ).start()

        return 0

    lax.fori_loop(0, slots * n_z, send_p, 0)
    combine(n_z - 1)

    pltpu.make_async_copy(dq_in.at[pl.ds(1, n_z - 1)], dq_in.at[pl.ds(1, n_z - 1)], dq_recv).wait()
    total = own_half[0]
    for i in range(1, n_z):
        total = total + dq_in[i].astype(F32)
    oq_ref[...] = total.astype(BF16)

    def settle(buf, n, sem):
        pltpu.make_async_copy(buf.at[pl.ds(0, n)], buf.at[pl.ds(0, n)], sem).wait()

    @pl.when(to_self)
    def _():
        settle(p_in, n_h - 1, p_recv)

    @pl.when(jnp.logical_not(to_self))
    def _():
        settle(p_in, n_h, p_recv)

    wide[...] = p_in[...].astype(F32).reshape(n_h * 2 * dr, LANES)
    for which, ref in enumerate((ok_ref, ov_ref)):
        picked = [wide[pl.ds(which * dr + d, n_h, stride=2 * dr), :] for d in range(dr)]
        ref[...] = jnp.concatenate(picked, 0).T.astype(BF16)

    for way in (0, 1):
        near(way).wait_send()
        fourth(way).wait_send()
        for half in (0, 1):
            far(way, half).wait_send()
            third(way, half).wait_send()
    for i in range(n_z):
        pair(i).wait_send()
        swap_half(i).wait_send()
    settle(dq_out, n_z - 1, dq_send)

    @pl.when(to_self)
    def _():
        settle(p_out, slots * n_z - 1, p_send)
        settle(kvs, n_h - 1, kv_send)

    @pl.when(jnp.logical_not(to_self))
    def _():
        settle(p_out, slots * n_z, p_send)

    @pl.when(is_source & (serves != c))
    def _():
        settle(kvs, n_h, kv_send)


def on_device(kv_states, queries_t, grad_out_t, log_norm, delta, lengths):
    n_z, n_s = lax.axis_size("grp"), lax.axis_size("seq")
    n_h = n_s // 2
    rows, cols = kv_states.shape
    tokens = queries_t.shape[1]
    slots = n_h // n_z
    keys = slots * rows
    dr = DH // n_z
    hbm = pl.BlockSpec(memory_space=pl.ANY)
    vmem = pl.BlockSpec(memory_space=pltpu.VMEM)
    dma = pltpu.SemaphoreType.DMA
    return pl.pallas_call(
        functools.partial(kernel, n_z, n_h, rows * n_s),
        out_shape=(
            jax.ShapeDtypeStruct((HALF, tokens), BF16),
            jax.ShapeDtypeStruct((rows, dr * n_h), BF16),
            jax.ShapeDtypeStruct((rows, dr * n_h), BF16),
        ),
        in_specs=[hbm] * 5 + [pl.BlockSpec(memory_space=pltpu.SMEM)],
        out_specs=(vmem,) * 3,
        scratch_shapes=[
            pltpu.VMEM((rows, cols), BF16),
            pltpu.VMEM((n_h, tokens), F32),
            pltpu.VMEM((n_h, tokens), F32),
            pltpu.VMEM((n_h, rows, LANES), BF16),
            pltpu.VMEM((slots, rows, LANES), BF16),
            pltpu.VMEM((n_z, 2, PART, tokens), BF16),
            pltpu.VMEM((2, keys, 2 * PART), BF16),
            pltpu.VMEM((DH, keys), BF16),
            pltpu.VMEM((keys, 2 * DH), F32),
            pltpu.VMEM((n_z, HALF, tokens), F32),
            pltpu.VMEM((n_z, HALF, tokens), F32),
            pltpu.VMEM((n_z, HALF, tokens), F32),
            pltpu.VMEM((n_z, HALF, tokens), BF16),
            pltpu.VMEM((n_z, HALF, tokens), BF16),
            pltpu.VMEM((slots * n_z, 2 * dr, LANES), BF16),
            pltpu.VMEM((n_h, 2 * dr, LANES), BF16),
            pltpu.VMEM((n_h * 2 * dr, LANES), F32),
            dma((5,)),
            dma, dma((slots,)),
            dma((2,)), dma((2,)),
            dma((2, 2)), dma((2, 2)),
            dma((2, 2)), dma((2, 2)),
            dma((2,)), dma((2,)),
            dma((n_z,)), dma((n_z,)),
            dma((n_z,)), dma((n_z,)),
            dma, dma, dma, dma,
        ],
        compiler_params=pltpu.CompilerParams(
            collective_id=0, has_side_effects=True, vmem_limit_bytes=63 * 1024 * 1024
        ),
        cost_estimate=pl.CostEstimate(
            flops=10 * DH * keys * tokens * n_z,
            bytes_accessed=4 * 1024 * 1024,
            transcendentals=keys * tokens * n_z,
        ),
    )(kv_states, queries_t, grad_out_t, log_norm, delta, lengths)


def solution(mesh):
    placed = (
        P("seq", None),
        P("seq", "grp"),
        P("seq", "grp"),
        P(None, "grp"),
        P(None, "grp"),
        P("grp"),
    )
    return jax.shard_map(
        on_device,
        mesh=mesh,
        in_specs=placed,
        out_specs=(P("seq", "grp"), P("seq", "grp"), P("seq", "grp")),
        check_vma=False,
    )
```

time: 58.5 us -> 50.1 us (0.86)
  Pallas kernels: 50.5 us -> 46.3 us
  local copies, waits for them, and re-layouts: 6.94 us -> 2.9 us
    pallas_call x1, Pallas kernels: 50.5 us -> 46.3 us  [on_device(): pl.pallas_call(functools.partial(kernel, n_z, n_h, rows * n_s), out_shape...]
    unnamed x15 -> x7, local copies, waits for them, and re-layouts: 6.94 us -> 2.9 us
where the time goes in v2:
time: 50.1 us; the launch traced here: 49.9 us
  Pallas kernels  46.3 us (92%)
  local copies, waits for them, and re-layouts  2.9 us (6%)
  between operations  0.65 us (1%)
    pallas_call x1, Pallas kernels, on_device(): pl.pallas_call(functools.partial(kernel, n_z, n_h, rows * n_s), out_shape...  46.3 us
    unnamed x7, local copies, waits for them, and re-layouts  2.9 us

profile of v2, /device:TPU:1, one launch (start us, length us, event | category | flops | bytes accessed | tf_op | source)
XLA Modules:
  0.0 49.9 jit_solution(1069866522536332662)
XLA Ops:
  0.6 46.3 %shard_map.85 = (bf16[32,512]{1,0:T(8,128)(2,1)}, bf16[128,256]{1,0:T(8,128)(2,1)}, bf16[128,256]{1,0:T(8,128)(2,1)}) custom-call(bf16[128,4096]{1,0:T(8,128)(2,1)} %kv_hbm.1, bf16[32,512]{1,0:T(8,128)(2,1)} %q_hbm.1, bf16[32,512]{1,0:T(8,128)(2,1)} %g_hbm.1, f32[32,512]{1,0:T(8,128)} %ln_hbm.1, f32[32,512]{1,0:T(8,128)} %dl_hbm.1, s32[2]{0:T(128)} %len_ref.1), custom_call_target="tpu_custom_call" | custom-call | flops 1342177280 | bytes 4194304 | tf_op jit(solution)/shard_map/pallas_call | solution.py:415
  47.0 0.0 copy-start.1
  47.0 1.4 %copy.12 = bf16[32,512]{1,0:T(8,128)(2,1)} copy(bf16[32,512]{1,0:T(8,128)(2,1)} %get-tuple-element.6) | data formatting | bytes 65536
  48.4 0.0 copy-done.1
  48.4 0.0 copy-start
  48.4 0.6 %copy.13 = bf16[128,256]{1,0:T(8,128)(2,1)} copy(bf16[128,256]{1,0:T(8,128)(2,1)S(1)} %copy-done.1) | data formatting | bytes 131072
  49.0 0.2 copy-done
  49.3 0.6 %copy.14 = bf16[128,256]{1,0:T(8,128)(2,1)} copy(bf16[128,256]{1,0:T(8,128)(2,1)S(1)} %copy-done) | data formatting | bytes 131072
Async XLA Ops:
  47.0 1.4 %copy-start.1 = (bf16[128,256]{1,0:T(8,128)(2,1)S(1)}, bf16[128,256]{1,0:T(8,128)(2,1)}, u32[]{:S(2)}) copy-start(bf16[128,256]{1,0:T(8,128)(2,1)} %get-tuple-element.7) | copy-start | bytes 196612
  48.4 0.9 %copy-start = (bf16[128,256]{1,0:T(8,128)(2,1)S(1)}, bf16[128,256]{1,0:T(8,128)(2,1)}, u32[]{:S(2)}) copy-start(bf16[128,256]{1,0:T(8,128)(2,1)} %get-tuple-element.8) | copy-start | bytes 196612

commit v3 on v2

--- a/solution.py
+++ b/solution.py
@@ -47,9 +47,9 @@
 def kernel(
     n_z, n_h, keys_all,
     kv_hbm, q_hbm, g_hbm, ln_hbm, dl_hbm, len_ref,
-    oq_ref, ok_ref, ov_ref,
+    oq_ref, op_ref,
     kvx, lnv, dlv, kvs, kvb, blocks, lhs, keys_t, acc,
-    own_half, sent_half, got_half, dq_out, dq_in, p_out, p_in, wide,
+    dq_sum, own_half, sent_half, got_half, dq_out, dq_in, p_out, p_in,
     in_sem, kv_send, kv_recv, near_send, near_recv, far_send, far_recv,
     third_send, third_recv, fourth_send, fourth_recv, pair_send, pair_recv,
     half_send, half_recv, dq_send, dq_recv, p_send, p_recv,
@@ -63,20 +63,28 @@
     tokens = blocks.shape[3]
     span = tokens // 2
     slots = kvb.shape[0]
-    keys = slots * rows
+    chunk = slots * rows // 2
     dr = DH // n_z
 
     width = n_z // 2
+    runs = n_h // width
     run = h // width
-    is_source = (lax.rem(h - run + n_h * width, width) == z // 2) & (c == lax.rem(z, 2))
-    serves = lax.rem(run, 2)
-
-    def source(slot):
-        at = 2 * slot + c
-        return 2 * (at * width + lax.rem(z // 2 + at, width)) + lax.rem(z, 2)
-
-    own_slot = run // 2
-    to_self = is_source & (serves == c)
+    turn = z // 2
+    is_source = c == lax.rem(z, 2)
+    to_self = (z == 0) & (c == 0)
+
+    def choose(table, i):
+        out = jnp.int32(table[-1])
+        for k in range(len(table) - 1):
+            out = jnp.where(i == k, table[k], out)
+        return out
+
+    def chip_at(away, along_run):
+        return lax.rem(run + away, runs) * width + lax.rem(h - run * width + along_run, width)
+
+    def source(place):
+        away = jnp.where(c == 0, choose((0, 2, 6, 4), place), choose((1, 7, 3, 5), place))
+        return 2 * chip_at(away, turn + away) + lax.rem(z, 2)
 
     barrier = pltpu.get_barrier_semaphore()
 
@@ -84,7 +92,7 @@
         pl.semaphore_signal(barrier, inc=1, device_id=device, device_id_type=MESH)
 
     def greet_source(i, _):
-        @pl.when(source(i) != s)
+        @pl.when(jnp.logical_not(to_self & (i == 0)))
         def _():
             greet((z, source(i)))
 
@@ -144,11 +152,11 @@
 
         lax.fori_loop(0, rows // STATS, sort, 0)
 
-        @pl.when(serves == c)
-        def _():
-            kvb[pl.ds(own_slot, 1)] = kvs[pl.ds(h, 1)]
-
-    served = jnp.where(is_source, n_h - jnp.where(serves == c, 1, 0), 0)
+        @pl.when(to_self)
+        def _():
+            kvb[0] = kvs[h]
+
+    served = jnp.where(is_source, runs - jnp.where(to_self, 1, 0), 0)
     pl.semaphore_wait(barrier, n_z + served)
 
     every = pl.ds(0, tokens)
@@ -194,25 +202,24 @@
         near(way).start()
     pair(0).start()
 
-    def kv_copy(to):
-        return pltpu.make_async_remote_copy(
-            src_ref=kvs.at[to], dst_ref=kvb.at[own_slot],
-            send_sem=kv_send, recv_sem=kv_recv.at[own_slot],
-            device_id=(z, 2 * to + serves), device_id_type=MESH,
-        )
-
     def send_kv(i, _):
-        to = lax.rem(h + n_h // 2 + i, n_h)
-
-        @pl.when(2 * to + serves != s)
-        def _():
-            kv_copy(to).start()
+        away = lax.rem(i + runs // 2, runs)
+        to = chip_at(runs - away, 2 * runs - turn - away)
+        place = choose((0, 0, 1, 2, 3, 3, 2, 1), away)
+
+        @pl.when(jnp.logical_not(to_self & (away == 0)))
+        def _():
+            pltpu.make_async_remote_copy(
+                src_ref=kvs.at[to], dst_ref=kvb.at[place],
+                send_sem=kv_send, recv_sem=kv_recv.at[place],
+                device_id=(z, 2 * to + lax.rem(away, 2)), device_id_type=MESH,
+            ).start()
 
         return 0
 
     @pl.when(is_source)
     def _():
-        lax.fori_loop(0, n_h, send_kv, 0)
+        lax.fori_loop(0, runs, send_kv, 0)
 
     lane = lax.broadcasted_iota(jnp.int32, (LANES, 2 * PART), 0)
     channel = lax.rem(lane, n_h) * (LANES // n_h) + lane // n_h
@@ -246,16 +253,20 @@
     for way in (0, 1):
         pair(3 + way).start()
 
-    for slot in range(slots):
-
-        @pl.when(jnp.logical_not(to_self & (own_slot == slot)))
-        def _():
-            pltpu.make_async_copy(kvb.at[slot], kvb.at[slot], kv_recv.at[slot]).wait()
-
-    mixed = kvb[...].reshape(keys, LANES)
-    lhs[0] = (dot(mixed, for_scores) + ones_s).astype(BF16)
-    lhs[1] = (dot(mixed, for_dprobs) + ones_p).astype(BF16)
-    keys_t[...] = dot(for_keys, mixed, NT).astype(BF16)
+    def keys_in(part):
+        for place in (part * slots // 2, part * slots // 2 + 1):
+
+            @pl.when(jnp.logical_not(to_self & (place == 0)))
+            def _():
+                pltpu.make_async_copy(kvb.at[place], kvb.at[place], kv_recv.at[place]).wait()
+
+        at = pl.ds(part * chunk, chunk)
+        mixed = kvb[pl.ds(part * slots // 2, slots // 2)].reshape(chunk, LANES)
+        lhs[0, at] = (dot(mixed, for_scores) + ones_s).astype(BF16)
+        lhs[1, at] = (dot(mixed, for_dprobs) + ones_p).astype(BF16)
+        keys_t[part] = dot(for_keys, mixed, NT).astype(BF16)
+
+    keys_in(0)
 
     def swap_half(i):
         return pltpu.make_async_remote_copy(
@@ -280,79 +291,108 @@
         def _():
             dq_copy(i).start()
 
-    chunk = min(keys, 256)
-
-    def compute(i, _):
-        @pl.when(i == 3)
+    def send_keys(part):
+        turned = acc[part * chunk : (part + 1) * chunk].T.reshape(2, n_z, dr, chunk)
+        first = part * slots // 2
+        for place in range(slots // 2):
+            columns = slice(place * rows, (place + 1) * rows)
+            for g in range(n_z):
+                tile = jnp.concatenate([turned[0, g, :, columns], turned[1, g, :, columns]], 0)
+                p_out[(first + place) * n_z + g] = tile.astype(BF16)
+        if part == 0:
+
+            @pl.when(to_self)
+            def _():
+                p_in[pl.ds(h, 1)] = p_out[pl.ds(z, 1)]
+
+        def send(i, _):
+            place = first + i // n_z
+            g = lax.rem(z + n_z // 2 + i, n_z)
+
+            @pl.when(jnp.logical_not(to_self & (place == 0) & (g == z)))
+            def _():
+                pltpu.make_async_remote_copy(
+                    src_ref=p_out.at[place * n_z + g], dst_ref=p_in.at[h],
+                    send_sem=p_send, recv_sem=p_recv,
+                    device_id=(g, source(place)), device_id_type=MESH,
+                ).start()
+
+            return 0
+
+        lax.fori_loop(0, slots // 2 * n_z, send, 0)
+
+    table_part = (0, 0, 0, 1, 1, 1, 1, 1, 0, 1, 0, 1, 0, 1, 0, 0)
+    table_step = (3, 4, 0, 3, 4, 0, 1, 2, 5, 5, 6, 6, 7, 7, 1, 2)
+    table_ends = (0, 0, 0, 1, 1, 1, 0, 0, 0, 1, 0, 1, 0, 1, 1, 1)
+
+    def compute(j, _):
+        part = choose(table_part, j)
+        i = choose(table_step, j)
+        opens = choose(table_ends, j) == 0
+
+        @pl.when(j == 3)
+        def _():
+            keys_in(1)
+
+        @pl.when(j == 5)
         def _():
             for way in (0, 1):
                 for half in (0, 1):
                     third(way, half).wait_recv()
                 pair(5 + way).start()
 
-        @pl.when(i == 5)
+        @pl.when(j == 7)
         def _():
             for way in (0, 1):
                 fourth(way).wait_recv()
             pair(7).start()
 
+        @pl.when(j == 14)
+        def _():
+            send_keys(1)
+
         block = order(i)
-        pltpu.make_async_copy(
-            blocks.at[block, 1 - c], blocks.at[block, 1 - c], pair_recv.at[i]
-        ).wait()
+
+        @pl.when(opens)
+        def _():
+            pltpu.make_async_copy(
+                blocks.at[block, 1 - c], blocks.at[block, 1 - c], pair_recv.at[i]
+            ).wait()
+
         rhs = blocks[block].reshape(2 * PART, tokens)
         blank = jnp.zeros((DH, tokens), BF16)
         q_rows = jnp.concatenate([rhs[:HALF], rhs[PART : PART + HALF], blank], 0)
         g_rows = jnp.concatenate([blank, rhs[HALF:DH], rhs[PART + HALF : PART + DH]], 0)
-        dq = jnp.zeros((DH, tokens), F32)
-        for k in range(0, keys, chunk):
-            part = slice(k, k + chunk)
-            probs = jnp.exp(dot(lhs[0, part], rhs))
-            dscores = probs * dot(lhs[1, part], rhs)
-            probs = probs.astype(BF16)
-            dscores = dscores.astype(BF16)
-            acc[part] += dot(dscores, q_rows, NT) + dot(probs, g_rows, NT)
-            dq += dot(keys_t[:, part], dscores)
-        top, bottom = dq[:HALF], dq[HALF:]
-        own_half[i] = jnp.where(c == 0, top, bottom)
-        sent_half[i] = jnp.where(c == 0, bottom, top)
-        swap_half(i).start()
-
-        @pl.when(i > 0)
-        def _():
-            combine(i - 1)
+        at = pl.ds(pl.multiple_of(part * chunk, chunk), chunk)
+        probs = jnp.exp(dot(lhs[0, at], rhs))
+        dscores = probs * dot(lhs[1, at], rhs)
+        probs = probs.astype(BF16)
+        dscores = dscores.astype(BF16)
+        acc[at] += dot(dscores, q_rows, NT) + dot(probs, g_rows, NT)
+        dq = dot(keys_t[part], dscores)
+
+        @pl.when(opens)
+        def _():
+            dq_sum[i] = dq
+
+        @pl.when(jnp.logical_not(opens))
+        def _():
+            total = dq_sum[i] + dq
+            top, bottom = total[:HALF], total[HALF:]
+            own_half[i] = jnp.where(c == 0, top, bottom)
+            sent_half[i] = jnp.where(c == 0, bottom, top)
+            swap_half(i).start()
+
+        @pl.when((j >= 2) & (choose(table_ends, j - 2) == 1))
+        def _():
+            combine(choose(table_step, j - 2))
 
         return 0
 
-    lax.fori_loop(0, n_z, compute, 0)
-
-    turned = acc[...].T.reshape(2, n_z, dr, keys)
-    for slot in range(slots):
-        columns = slice(slot * rows, (slot + 1) * rows)
-        for g in range(n_z):
-            tile = jnp.concatenate([turned[0, g, :, columns], turned[1, g, :, columns]], 0)
-            p_out[slot * n_z + g] = tile.astype(BF16)
-
-    @pl.when(to_self)
-    def _():
-        p_in[pl.ds(h, 1)] = p_out[pl.ds(own_slot * n_z + z, 1)]
-
-    def send_p(i, _):
-        slot = lax.rem(i // n_z + h, slots)
-        g = lax.rem(z + n_z // 2 + i, n_z)
-
-        @pl.when((g != z) | (source(slot) != s))
-        def _():
-            pltpu.make_async_remote_copy(
-                src_ref=p_out.at[slot * n_z + g], dst_ref=p_in.at[h],
-                send_sem=p_send, recv_sem=p_recv,
-                device_id=(g, source(slot)), device_id_type=MESH,
-            ).start()
-
-        return 0
-
-    lax.fori_loop(0, slots * n_z, send_p, 0)
-    combine(n_z - 1)
+    lax.fori_loop(0, 2 * n_z, compute, 0)
+    send_keys(0)
+    combine(table_step[-2])
+    combine(table_step[-1])
 
     pltpu.make_async_copy(dq_in.at[pl.ds(1, n_z - 1)], dq_in.at[pl.ds(1, n_z - 1)], dq_recv).wait()
     total = own_half[0]
@@ -371,10 +411,7 @@
     def _():
         settle(p_in, n_h, p_recv)
 
-    wide[...] = p_in[...].astype(F32).reshape(n_h * 2 * dr, LANES)
-    for which, ref in enumerate((ok_ref, ov_ref)):
-        picked = [wide[pl.ds(which * dr + d, n_h, stride=2 * dr), :] for d in range(dr)]
-        ref[...] = jnp.concatenate(picked, 0).T.astype(BF16)
+    op_ref[...] = p_in[...]
 
     for way in (0, 1):
         near(way).wait_send()
@@ -390,15 +427,25 @@
     @pl.when(to_self)
     def _():
         settle(p_out, slots * n_z - 1, p_send)
-        settle(kvs, n_h - 1, kv_send)
+        settle(kvs, runs - 1, kv_send)
 
     @pl.when(jnp.logical_not(to_self))
     def _():
         settle(p_out, slots * n_z, p_send)
 
-    @pl.when(is_source & (serves != c))
-    def _():
-        settle(kvs, n_h, kv_send)
+    @pl.when(is_source & jnp.logical_not(to_self))
+    def _():
+        settle(kvs, runs, kv_send)
+
+
+def last_kernel(q_ref, p_ref, oq_ref, ok_ref, ov_ref, wide):
+    n_h, both, _ = p_ref.shape
+    dr = both // 2
+    oq_ref[...] = q_ref[...]
+    wide[...] = p_ref[...].astype(F32).reshape(n_h * both, LANES)
+    for which, ref in enumerate((ok_ref, ov_ref)):
+        picked = [wide[pl.ds(which * dr + d, n_h, stride=both), :] for d in range(dr)]
+        ref[...] = jnp.concatenate(picked, 0).T.astype(BF16)
 
 
 def on_device(kv_states, queries_t, grad_out_t, log_norm, delta, lengths):
@@ -412,15 +459,14 @@
     hbm = pl.BlockSpec(memory_space=pl.ANY)
     vmem = pl.BlockSpec(memory_space=pltpu.VMEM)
     dma = pltpu.SemaphoreType.DMA
-    return pl.pallas_call(
+    grad_query, tiles = pl.pallas_call(
         functools.partial(kernel, n_z, n_h, rows * n_s),
         out_shape=(
             jax.ShapeDtypeStruct((HALF, tokens), BF16),
-            jax.ShapeDtypeStruct((rows, dr * n_h), BF16),
-            jax.ShapeDtypeStruct((rows, dr * n_h), BF16),
+            jax.ShapeDtypeStruct((n_h, 2 * dr, LANES), BF16),
         ),
         in_specs=[hbm] * 5 + [pl.BlockSpec(memory_space=pltpu.SMEM)],
-        out_specs=(vmem,) * 3,
+        out_specs=(vmem,) * 2,
         scratch_shapes=[
             pltpu.VMEM((rows, cols), BF16),
             pltpu.VMEM((n_h, tokens), F32),
@@ -429,8 +475,9 @@
             pltpu.VMEM((slots, rows, LANES), BF16),
             pltpu.VMEM((n_z, 2, PART, tokens), BF16),
             pltpu.VMEM((2, keys, 2 * PART), BF16),
-            pltpu.VMEM((DH, keys), BF16),
+            pltpu.VMEM((2, DH, keys // 2), BF16),
             pltpu.VMEM((keys, 2 * DH), F32),
+            pltpu.VMEM((n_z, DH, tokens), F32),
             pltpu.VMEM((n_z, HALF, tokens), F32),
             pltpu.VMEM((n_z, HALF, tokens), F32),
             pltpu.VMEM((n_z, HALF, tokens), F32),
@@ -438,7 +485,6 @@
             pltpu.VMEM((n_z, HALF, tokens), BF16),
             pltpu.VMEM((slots * n_z, 2 * dr, LANES), BF16),
             pltpu.VMEM((n_h, 2 * dr, LANES), BF16),
-            pltpu.VMEM((n_h * 2 * dr, LANES), F32),
             dma((5,)),
             dma, dma((slots,)),
             dma((2,)), dma((2,)),
@@ -458,6 +504,17 @@
             transcendentals=keys * tokens * n_z,
         ),
     )(kv_states, queries_t, grad_out_t, log_norm, delta, lengths)
+    return pl.pallas_call(
+        last_kernel,
+        out_shape=(
+            jax.ShapeDtypeStruct((HALF, tokens), BF16),
+            jax.ShapeDtypeStruct((rows, dr * n_h), BF16),
+            jax.ShapeDtypeStruct((rows, dr * n_h), BF16),
+        ),
+        in_specs=[vmem] * 2,
+        out_specs=(vmem,) * 3,
+        scratch_shapes=[pltpu.VMEM((n_h * 2 * dr, LANES), F32)],
+    )(grad_query, tiles)
 
 
 def solution(mesh):

time: 50.1 us -> 46.2 us (0.922)
  local copies, waits for them, and re-layouts: 2.9 us -> 0 us
  Pallas kernels: 46.3 us -> 45.4 us
    unnamed x7 -> x0, local copies, waits for them, and re-layouts: 2.9 us -> none
    pallas_call x1, Pallas kernels: 46.3 us -> 43.6 us  [on_device(): pl.pallas_call(functools.partial(kernel, n_z, n_h, rows * n_s), out_shape...]
    pallas_call x0 -> x1, Pallas kernels: none -> 1.73 us  [on_device(): pl.pallas_call(last_kernel, out_shape=(jax.ShapeDtypeStruct((HALF, tokens...]
where the time goes in v3:
time: 46.2 us; the launch traced here: 46 us
  Pallas kernels  45.4 us (98%)
  between operations  0.64 us (1%)
    pallas_call x1, Pallas kernels, on_device(): pl.pallas_call(functools.partial(kernel, n_z, n_h, rows * n_s), out_shape...  43.6 us
    pallas_call x1, Pallas kernels, on_device(): pl.pallas_call(last_kernel, out_shape=(jax.ShapeDtypeStruct((HALF, tokens...  1.73 us

profile of v3, /device:TPU:1, one launch (start us, length us, event | category | flops | bytes accessed | tf_op | source)
XLA Modules:
  0.0 46.0 jit_solution(15734856741671127509)
XLA Ops:
  0.6 43.6 %shard_map.85 = (bf16[32,512]{1,0:T(8,128)(2,1)}, bf16[32,16,128]{2,1,0:T(8,128)(2,1)}) custom-call(bf16[128,4096]{1,0:T(8,128)(2,1)} %kv_hbm.1, bf16[32,512]{1,0:T(8,128)(2,1)} %q_hbm.1, bf16[32,512]{1,0:T(8,128)(2,1)} %g_hbm.1, f32[32,512]{1,0:T(8,128)} %ln_hbm.1, f32[32,512]{1,0:T(8,128)} %dl_hbm.1, s32[2]{0:T(128)} %len_ref.1), custom_call_target="tpu_custom_call" | custom-call | flops 1342177280 | bytes 4194304 | tf_op jit(solution)/shard_map/pallas_call | solution.py:462
  44.3 1.7 %shard_map.86 = (bf16[32,512]{1,0:T(8,128)(2,1)}, bf16[128,256]{1,0:T(8,128)(2,1)}, bf16[128,256]{1,0:T(8,128)(2,1)}) custom-call(bf16[32,512]{1,0:T(8,128)(2,1)} %get-tuple-element.5.q_ref, bf16[32,16,128]{2,1,0:T(8,128)(2,1)} %get-tuple-element.6.p_ref), custom_call_target="tpu_custom_call" | custom-call | tf_op jit(solution)/shard_map/pallas_call | solution.py:507

commit v4 on v3

v4 whole, which is shorter than its diff:
```python
import functools
import math

import jax
import jax.numpy as jnp
from jax import lax
from jax.experimental import pallas as pl
from jax.experimental.pallas import tpu as pltpu
from jax.sharding import PartitionSpec as P

DH = 64
LEN = 256
HALF = DH // 2
STATS = 16
PART = 2 * HALF
DEPTH = 2 * PART + STATS
LANES = 128
MESH = pl.DeviceIdType.MESH
F32 = jnp.float32
BF16 = jnp.bfloat16

AWAY = (
    ((4, 3), (3, 2), (5, 2), (4, 2)),
    ((3, 3), (5, 1), (6, 2), (4, 1)),
    ((3, 1), (5, 3), (2, 2), (4, 0)),
    ((2, 3), (6, 1), (7, 2), (5, 0)),
    ((2, 1), (6, 3), (1, 2), (3, 0)),
    ((1, 1), (1, 3), (7, 1), (7, 3)),
    ((7, 0), (0, 2), (2, 0), (6, 0)),
    ((0, 0), (0, 1), (0, 3), (1, 0)),
)

NT = (((1,), (1,)), ((), ()))
NN = (((1,), (0,)), ((), ()))


def dot(a, b, dims=NN):
    return lax.dot_general(a, b, dims, preferred_element_type=F32)


def exchange_lanes(tiles, unit):
    count = len(tiles)
    lane = lax.broadcasted_iota(jnp.int32, tiles[0].shape, 1)
    step = 1
    while step < count:
        shift = step * unit
        low = (lane & shift) == 0
        made = list(tiles)
        for a in range(count):
            if a & step == 0:
                x, y = tiles[a], tiles[a | step]
                made[a] = jnp.where(low, x, pltpu.roll(y, shift, 1))
                made[a | step] = jnp.where(low, pltpu.roll(x, LANES - shift, 1), y)
        tiles = made
        step *= 2
    return tiles


def kernel(
    n_z, n_h, keys_all,
    kv_hbm, q_hbm, g_hbm, ln_hbm, dl_hbm, len_hbm,
    oq_ref, op_ref,
    kvx, lnv, dlv, len_ref, stored, stats, kvs, kvb, blocks, lhs, keys_t, acc,
    dq_sum, own_half, sent_half, got_half, dq_out, dq_in, p_out, dq_done,
    in_sem, out_sem, stat_send, stat_recv, kv_send, kv_recv, near_send, near_recv, far_send, far_recv,
    third_send, third_recv, fourth_send, fourth_recv, pair_send, pair_recv,
    half_send, half_recv, dq_send, dq_recv, p_send, p_recv,
):
    z = lax.axis_index("grp")
    s = lax.axis_index("seq")
    h = s // 2
    c = s - 2 * h
    partner = 2 * h + 1 - c
    rows = kvx.shape[0]
    tokens = blocks.shape[3]
    span = tokens // 2
    slots = kvb.shape[0]
    chunk = slots * rows // 2
    dr = DH // n_z

    width = n_z // 2
    runs = n_h // width
    run = h // width
    along_run = h - run * width
    to_self = z == n_z - 1

    def choose(table, i):
        out = jnp.int32(table[-1])
        for k in range(len(table) - 1):
            out = jnp.where(i == k, table[k], out)
        return out

    sources, served = [], []
    for place in range(slots):
        down = choose([AWAY[k][place][0] for k in range(n_z)], z)
        right = choose([AWAY[k][place][1] for k in range(n_z)], z)
        sources.append(lax.rem(run + down, runs) * width + lax.rem(along_run + right, width))
        served.append(
            lax.rem(run + runs - down, runs) * width + lax.rem(along_run + width - right, width)
        )

    def unless_self(place, go):
        if place == 0:
            pl.when(jnp.logical_not(to_self))(go)
        else:
            go()

    barrier = pltpu.get_barrier_semaphore()

    def greet(device):
        pl.semaphore_signal(barrier, inc=1, device_id=device, device_id_type=MESH)

    def greet_line(i, _):
        greet((lax.rem(z + i, n_z), s))
        return 0

    for place in range(slots):
        unless_self(place, functools.partial(greet, (z, 2 * sources[place] + c)))
    lax.fori_loop(1, n_z, greet_line, 0)
    greet((z, partner))

    loads = [
        pltpu.make_async_copy(ln_hbm, lnv, in_sem.at[0]),
        pltpu.make_async_copy(dl_hbm, dlv, in_sem.at[1]),
        pltpu.make_async_copy(q_hbm, blocks.at[z, c, pl.ds(0, HALF)], in_sem.at[2]),
        pltpu.make_async_copy(g_hbm, blocks.at[z, c, pl.ds(HALF, HALF)], in_sem.at[3]),
    ]
    for load in loads:
        load.start()
    load_lengths = pltpu.make_async_copy(len_hbm, len_ref, in_sem.at[5])
    load_lengths.start()
    load_kv = pltpu.make_async_copy(kv_hbm, kvx, in_sem.at[4])

    load_kv.start()

    loads[0].wait()
    loads[1].wait()
    load_lengths.wait()
    place = lax.broadcasted_iota(jnp.int32, (1, tokens), 1)
    limit = jnp.zeros((1, tokens), jnp.int32)
    for a in range(tokens // LEN):
        limit = jnp.where(place // LEN == a, len_ref[a], limit)
    norm = -(lnv[pl.ds(h, 1), :] + math.log(keys_all))
    norm = jnp.where(lax.rem(place, LEN) < limit, norm, -1e30)
    less = -dlv[pl.ds(h, 1), :]
    for k in range(tokens // LANES):
        columns = slice(k * LANES, (k + 1) * LANES)
        stored[z, k : k + 1] = norm[:, columns]
        stored[z, tokens // LANES + k : tokens // LANES + k + 1] = less[:, columns]
    loads[2].wait()
    loads[3].wait()

    load_kv.wait()

    group = LANES // slots
    at = lax.broadcasted_iota(jnp.int32, (2 * LANES, LANES), 0)
    to = lax.broadcasted_iota(jnp.int32, (2 * LANES, LANES), 1)
    wanted = jnp.zeros_like(to)
    for place in range(slots):
        wanted = jnp.where(to // group == place, served[place], wanted)
    by_head = lax.rem(at, n_h) == wanted
    per = 2 * LANES // n_h
    picked = jnp.zeros((slots * rows, LANES), F32)
    for step in range(group // per):
        one_hot = by_head & (lax.rem(to, group) == step * per + at // n_h)
        taken = [
            kvx[:, (m * group // per + step) * 2 * LANES : (m * group // per + step + 1) * 2 * LANES]
            for m in range(slots)
        ]
        picked += dot(jnp.concatenate(taken, 0), jnp.where(one_hot, 1.0, 0.0).astype(BF16))
    tiles = exchange_lanes([picked[m * rows : (m + 1) * rows] for m in range(slots)], group)
    for place in range(slots):
        kvs[place] = tiles[place].astype(BF16)

    @pl.when(to_self)
    def _():
        kvb[0] = kvs[0]

    pl.semaphore_wait(barrier, n_z + slots - jnp.where(to_self, 1, 0))

    every = pl.ds(0, tokens)

    def columns_of(half):
        return pl.ds(pl.multiple_of(half * span, span), span)


    def order(i):
        t = (i + 1) // 2
        return lax.rem(jnp.where(lax.rem(i, 2) == 1, z - t, z + t) + n_z, n_z)

    def along(way, hops, block, columns, send, recv):
        to = lax.rem(z + jnp.where(way == 0, hops, n_z - hops), n_z)
        ref = blocks.at[block, c, :, columns]
        return pltpu.make_async_remote_copy(
            src_ref=ref, dst_ref=ref, send_sem=send, recv_sem=recv,
            device_id=(to, s), device_id_type=MESH,
        )

    def near(way):
        return along(way, 1, z, every, near_send.at[way], near_recv.at[way])

    def far(way, half):
        return along(way, 2, z, columns_of(half), far_send.at[way, half], far_recv.at[way, half])

    def third(way, half):
        block = order(3 + way)
        return along(way, 1, block, columns_of(half), third_send.at[way, half], third_recv.at[way, half])

    def fourth(way):
        return along(way, 2, order(3 + way), columns_of(way), fourth_send.at[way], fourth_recv.at[way])

    def pair(i):
        ref = blocks.at[order(i), c]
        return pltpu.make_async_remote_copy(
            src_ref=ref, dst_ref=ref,
            send_sem=pair_send.at[i], recv_sem=pair_recv.at[i],
            device_id=(z, partner), device_id_type=MESH,
        )

    for half in (0, 1):
        for way in (0, 1):
            far(way, half).start()

    def send_stored(i, _):
        pltpu.make_async_remote_copy(
            src_ref=stored.at[z], dst_ref=stored.at[z], send_sem=stat_send, recv_sem=stat_recv,
            device_id=(lax.rem(z + i, n_z), s), device_id_type=MESH,
        ).start()
        return 0

    for way in (0, 1):
        near(way).start()
    lax.fori_loop(1, n_z, send_stored, 0)
    pair(0).start()

    for place in reversed(range(slots)):
        copy = pltpu.make_async_remote_copy(
            src_ref=kvs.at[place], dst_ref=kvb.at[place],
            send_sem=kv_send.at[place], recv_sem=kv_recv.at[place],
            device_id=(z, 2 * served[place] + c), device_id_type=MESH,
        )
        unless_self(place, copy.start)

    lane = lax.broadcasted_iota(jnp.int32, (LANES, DEPTH), 0)
    col = lax.broadcasted_iota(jnp.int32, (LANES, DEPTH), 1)
    side = col // PART
    within = col - side * PART
    is_key = (side < 2) & (within < HALF)
    is_value = (side < 2) & (within >= HALF)
    for_scores = jnp.where(is_key & (lane == side * HALF + within), 1.0, 0.0).astype(BF16)
    for_dprobs = jnp.where(
        is_value & (lane == DH + side * HALF + within - HALF), 1.0, 0.0
    ).astype(BF16)
    one = lax.broadcasted_iota(jnp.int32, (1, DEPTH), 1) - 2 * PART
    ones_s = jnp.where((one >= 0) & (one < 3), 1.0, 0.0)
    ones_p = jnp.where((one >= 3) & (one < 6), 1.0, 0.0)
    lane_t = lax.broadcasted_iota(jnp.int32, (DH, LANES), 1)
    row_t = lax.broadcasted_iota(jnp.int32, (DH, LANES), 0)
    for_keys = jnp.where(lane_t == row_t, 1.0, 0.0).astype(BF16)
    acc[...] = jnp.zeros_like(acc)

    first_way = jnp.where((z >= n_z // 4) & (z < 3 * n_z // 4), 0, 1)
    for half in (0, 1):
        for way in (first_way, 1 - first_way):
            far(way, half).wait_recv()
            third(way, half).start()

            @pl.when(way == half)
            def _():
                fourth(way).start()

    for way in (0, 1):
        pair(3 + way).start()
    for way in (0, 1):
        near(way).wait_recv()
        pair(1 + way).start()

    pltpu.make_async_copy(stored.at[pl.ds(1, n_z - 1)], stored.at[pl.ds(1, n_z - 1)], stat_recv).wait()
    at = lax.broadcasted_iota(jnp.int32, (STATS, tokens), 0)

    def split(b, _):
        rows_of = tokens // LANES
        norm = jnp.concatenate([stored[b, k : k + 1] for k in range(rows_of)], 1)
        less = jnp.concatenate([stored[b, rows_of + k : rows_of + k + 1] for k in range(rows_of)], 1)
        both = jnp.where(at < 3, norm, less)
        high = both.astype(BF16).astype(F32)
        middle = (both - high).astype(BF16).astype(F32)
        low = both - high - middle
        which = lax.rem(at, 3)
        out = jnp.where(which == 0, high, jnp.where(which == 1, middle, low))
        stats[b] = jnp.where(at < 6, out, 0.0).astype(BF16)
        return 0

    lax.fori_loop(0, n_z, split, 0)

    def keys_in(part):
        for place in (part * slots // 2, part * slots // 2 + 1):

            arrived = pltpu.make_async_copy(kvb.at[place], kvb.at[place], kv_recv.at[place])
            unless_self(place, arrived.wait)

        at = pl.ds(part * chunk, chunk)
        mixed = kvb[pl.ds(part * slots // 2, slots // 2)].reshape(chunk, LANES)
        lhs[0, at] = (dot(mixed, for_scores) + ones_s).astype(BF16)
        lhs[1, at] = (dot(mixed, for_dprobs) + ones_p).astype(BF16)
        keys_t[part] = dot(for_keys, mixed, NT).astype(BF16)

    keys_in(0)

    def swap_half(i):
        return pltpu.make_async_remote_copy(
            src_ref=sent_half.at[i], dst_ref=got_half.at[i],
            send_sem=half_send.at[i], recv_sem=half_recv.at[i],
            device_id=(z, partner), device_id_type=MESH,
        )

    def dq_copy(i):
        return pltpu.make_async_remote_copy(
            src_ref=dq_out.at[i], dst_ref=dq_in.at[i], send_sem=dq_send, recv_sem=dq_recv,
            device_id=(order(i), s), device_id_type=MESH,
        )

    def combine(i):
        swap_half(i).wait_recv()
        total = own_half[i] + got_half[i]
        own_half[i] = total
        dq_out[i] = total.astype(BF16)

        @pl.when(i > 0)
        def _():
            dq_copy(i).start()

    own_tile = pltpu.make_async_copy(p_out.at[z], op_ref.at[h], out_sem.at[0])
    out_query = pltpu.make_async_copy(dq_done, oq_ref, out_sem.at[1])

    def send_keys(part):
        turned = acc[part * chunk : (part + 1) * chunk].T.reshape(2, n_z, dr, chunk)
        first = part * slots // 2
        for place in range(slots // 2):
            columns = slice(place * rows, (place + 1) * rows)
            for g in range(n_z):
                tile = jnp.concatenate([turned[0, g, :, columns], turned[1, g, :, columns]], 0)
                p_out[(first + place) * n_z + g] = tile.astype(BF16)
        if part == 0:
            pl.when(to_self)(own_tile.start)

        for place in reversed(range(first, first + slots // 2)):

            def send(g, _):
                def go():
                    pltpu.make_async_remote_copy(
                        src_ref=p_out.at[place * n_z + g], dst_ref=op_ref.at[h],
                        send_sem=p_send, recv_sem=p_recv,
                        device_id=(g, 2 * sources[place] + c), device_id_type=MESH,
                    ).start()

                if place == 0:
                    pl.when(jnp.logical_not(to_self & (g == z)))(go)
                else:
                    go()
                return 0

            lax.fori_loop(0, n_z, send, 0)

    table_part = (0,) * 5 + (1,) * 8 + (0,) * 3
    table_step = (0, 1, 2, 3, 4, 0, 1, 2, 3, 4, 5, 6, 7, 5, 6, 7)
    table_ends = (0,) * 5 + (1,) * 5 + (0,) * 3 + (1,) * 3
    keys_at, third_at, fourth_at, far_done = 0, 5, 7, 13

    def compute(j, _):
        part = choose(table_part, j)
        i = choose(table_step, j)
        opens = choose(table_ends, j) == 0

        @pl.when(j == keys_at)
        def _():
            keys_in(1)

        @pl.when(j == third_at)
        def _():
            for way in (0, 1):
                for half in (0, 1):
                    third(way, half).wait_recv()
                pair(5 + way).start()

        @pl.when(j == fourth_at)
        def _():
            for way in (0, 1):
                fourth(way).wait_recv()
            pair(7).start()

        @pl.when(j == far_done)
        def _():
            send_keys(1)

        block = order(i)

        @pl.when(opens)
        def _():
            pltpu.make_async_copy(
                blocks.at[block, 1 - c], blocks.at[block, 1 - c], pair_recv.at[i]
            ).wait()

        rhs = jnp.concatenate([blocks[block].reshape(2 * PART, tokens), stats[block]], 0)
        blank = jnp.zeros((DH, tokens), BF16)
        q_rows = jnp.concatenate([rhs[:HALF], rhs[PART : PART + HALF], blank], 0)
        g_rows = jnp.concatenate([blank, rhs[HALF:PART], rhs[PART + HALF : 2 * PART]], 0)
        at = pl.ds(pl.multiple_of(part * chunk, chunk), chunk)
        probs = jnp.exp(dot(lhs[0, at], rhs))
        dscores = probs * dot(lhs[1, at], rhs)
        probs = probs.astype(BF16)
        dscores = dscores.astype(BF16)
        acc[at] += dot(dscores, q_rows, NT) + dot(probs, g_rows, NT)
        dq = dot(keys_t[part], dscores)

        @pl.when(opens)
        def _():
            dq_sum[i] = dq

        @pl.when(jnp.logical_not(opens))
        def _():
            total = dq_sum[i] + dq
            top, bottom = total[:HALF], total[HALF:]
            own_half[i] = jnp.where(c == 0, top, bottom)
            sent_half[i] = jnp.where(c == 0, bottom, top)
            swap_half(i).start()

        @pl.when((j >= 2) & (choose(table_ends, j - 2) == 1))
        def _():
            combine(choose(table_step, j - 2))

        return 0

    lax.fori_loop(0, 2 * n_z, compute, 0)
    send_keys(0)
    combine(table_step[-2])
    combine(table_step[-1])

    pltpu.make_async_copy(dq_in.at[pl.ds(1, n_z - 1)], dq_in.at[pl.ds(1, n_z - 1)], dq_recv).wait()
    total = own_half[0]
    for i in range(1, n_z):
        total = total + dq_in[i].astype(F32)
    dq_done[...] = total.astype(BF16)
    out_query.start()

    def settle(buf, n, sem):
        pltpu.make_async_copy(buf.at[pl.ds(0, n)], buf.at[pl.ds(0, n)], sem).wait()

    @pl.when(to_self)
    def _():
        settle(op_ref, n_h - 1, p_recv)
        own_tile.wait()

    @pl.when(jnp.logical_not(to_self))
    def _():
        settle(op_ref, n_h, p_recv)

    out_query.wait()

    for way in (0, 1):
        near(way).wait_send()
        fourth(way).wait_send()
        for half in (0, 1):
            far(way, half).wait_send()
            third(way, half).wait_send()
    for i in range(n_z):
        pair(i).wait_send()
        swap_half(i).wait_send()
    settle(dq_out, n_z - 1, dq_send)
    settle(stored, n_z - 1, stat_send)

    @pl.when(to_self)
    def _():
        settle(p_out, slots * n_z - 1, p_send)

    @pl.when(jnp.logical_not(to_self))
    def _():
        settle(p_out, slots * n_z, p_send)

    for place in range(slots):
        left = pltpu.make_async_copy(kvb.at[place], kvb.at[place], kv_send.at[place])
        unless_self(place, left.wait)


def last_kernel(q_ref, p_ref, oq_ref, ok_ref, ov_ref, wide):
    n_h, both, _ = p_ref.shape
    dr = both // 2
    oq_ref[...] = q_ref[...]
    wide[...] = p_ref[...].astype(F32).reshape(n_h * both, LANES)
    for which, ref in enumerate((ok_ref, ov_ref)):
        picked = [wide[pl.ds(which * dr + d, n_h, stride=both), :] for d in range(dr)]
        ref[...] = jnp.concatenate(picked, 0).T.astype(BF16)


def on_device(kv_states, queries_t, grad_out_t, log_norm, delta, lengths):
    n_z, n_s = lax.axis_size("grp"), lax.axis_size("seq")
    n_h = n_s // 2
    rows, cols = kv_states.shape
    tokens = queries_t.shape[1]
    slots = n_h // n_z
    keys = slots * rows
    dr = DH // n_z
    given = (kv_states, queries_t, grad_out_t, log_norm, delta, lengths)
    hbm = pl.BlockSpec(memory_space=pl.ANY)
    vmem = pl.BlockSpec(memory_space=pltpu.VMEM)
    dma = pltpu.SemaphoreType.DMA
    grad_query, tiles = pl.pallas_call(
        functools.partial(kernel, n_z, n_h, rows * n_s),
        out_shape=(
            jax.ShapeDtypeStruct((HALF, tokens), BF16),
            jax.ShapeDtypeStruct((n_h, 2 * dr, LANES), BF16),
        ),
        in_specs=[hbm] * 6,
        out_specs=(hbm,) * 2,
        scratch_shapes=[
            pltpu.VMEM((rows, cols), BF16),
            pltpu.VMEM((n_h, tokens), F32),
            pltpu.VMEM((n_h, tokens), F32),
            pltpu.SMEM(lengths.shape, jnp.int32),
            pltpu.VMEM((n_z, 2 * tokens // LANES, LANES), F32),
            pltpu.VMEM((n_z, STATS, tokens), BF16),
            pltpu.VMEM((slots, rows, LANES), BF16),
            pltpu.VMEM((slots, rows, LANES), BF16),
            pltpu.VMEM((n_z, 2, PART, tokens), BF16),
            pltpu.VMEM((2, keys, DEPTH), BF16),
            pltpu.VMEM((2, DH, keys // 2), BF16),
            pltpu.VMEM((keys, 2 * DH), F32),
            pltpu.VMEM((n_z, DH, tokens), F32),
            pltpu.VMEM((n_z, HALF, tokens), F32),
            pltpu.VMEM((n_z, HALF, tokens), F32),
            pltpu.VMEM((n_z, HALF, tokens), F32),
            pltpu.VMEM((n_z, HALF, tokens), BF16),
            pltpu.VMEM((n_z, HALF, tokens), BF16),
            pltpu.VMEM((slots * n_z, 2 * dr, LANES), BF16),
            pltpu.VMEM((HALF, tokens), BF16),
            dma((6,)), dma((2,)),
            dma, dma,
            dma((slots,)), dma((slots,)),
            dma((2,)), dma((2,)),
            dma((2, 2)), dma((2, 2)),
            dma((2, 2)), dma((2, 2)),
            dma((2,)), dma((2,)),
            dma((n_z,)), dma((n_z,)),
            dma((n_z,)), dma((n_z,)),
            dma, dma, dma, dma,
        ],
        compiler_params=pltpu.CompilerParams(
            collective_id=0, has_side_effects=True, vmem_limit_bytes=63 * 1024 * 1024
        ),
        cost_estimate=pl.CostEstimate(
            flops=10 * DH * keys * tokens * n_z,
            bytes_accessed=4 * 1024 * 1024,
            transcendentals=keys * tokens * n_z,
        ),
    )(*given)
    return pl.pallas_call(
        last_kernel,
        out_shape=(
            jax.ShapeDtypeStruct((HALF, tokens), BF16),
            jax.ShapeDtypeStruct((rows, dr * n_h), BF16),
            jax.ShapeDtypeStruct((rows, dr * n_h), BF16),
        ),
        in_specs=[vmem] * 2,
        out_specs=(vmem,) * 3,
        scratch_shapes=[pltpu.VMEM((n_h * 2 * dr, LANES), F32)],
    )(grad_query, tiles)


def solution(mesh):
    placed = (
        P("seq", None),
        P("seq", "grp"),
        P("seq", "grp"),
        P(None, "grp"),
        P(None, "grp"),
        P("grp"),
    )
    return jax.shard_map(
        on_device,
        mesh=mesh,
        in_specs=placed,
        out_specs=(P("seq", "grp"), P("seq", "grp"), P("seq", "grp")),
        check_vma=False,
    )
```

time: 46.2 us -> 43 us (0.931)
  Pallas kernels: 45.4 us -> 42.1 us
    pallas_call x1, Pallas kernels: 43.6 us -> 40.4 us  [on_device(): pl.pallas_call(functools.partial(kernel, n_z, n_h, rows * n_s), out_shape...]
where the time goes in v4:
time: 43 us; the launch traced here: 42.8 us
  Pallas kernels  42.1 us (98%)
  between operations  0.64 us (1%)
    pallas_call x1, Pallas kernels, on_device(): pl.pallas_call(functools.partial(kernel, n_z, n_h, rows * n_s), out_shape...  40.4 us
    pallas_call x1, Pallas kernels, on_device(): pl.pallas_call(last_kernel, out_shape=(jax.ShapeDtypeStruct((HALF, tokens...  1.73 us

profile of v4, /device:TPU:1, one launch (start us, length us, event | category | flops | bytes accessed | tf_op | source)
XLA Modules:
  0.0 42.8 jit_solution(18208039597652880137)
XLA Ops:
  0.6 40.4 %shard_map.85 = (bf16[32,512]{1,0:T(8,128)(2,1)}, bf16[32,16,128]{2,1,0:T(8,128)(2,1)}) custom-call(bf16[128,4096]{1,0:T(8,128)(2,1)} %kv_hbm.1, bf16[32,512]{1,0:T(8,128)(2,1)} %q_hbm.1, bf16[32,512]{1,0:T(8,128)(2,1)} %g_hbm.1, f32[32,512]{1,0:T(8,128)} %ln_hbm.1, f32[32,512]{1,0:T(8,128)} %dl_hbm.1, s32[2]{0:T(128)} %len_hbm.1), custom_call_target="tpu_custom_call" | custom-call | flops 1342177280 | bytes 4194304 | tf_op jit(solution)/shard_map/pallas_call | solution.py:507
  41.1 1.7 %shard_map.86 = (bf16[32,512]{1,0:T(8,128)(2,1)}, bf16[128,256]{1,0:T(8,128)(2,1)}, bf16[128,256]{1,0:T(8,128)(2,1)}) custom-call(bf16[32,512]{1,0:T(8,128)(2,1)} %get-tuple-element.5.q_ref, bf16[32,16,128]{2,1,0:T(8,128)(2,1)} %get-tuple-element.6.p_ref), custom_call_target="tpu_custom_call" | custom-call | tf_op jit(solution)/shard_map/pallas_call | solution.py:556

commit v5 on v4

--- a/solution.py
+++ b/solution.py
@@ -362,15 +362,19 @@
 
             lax.fori_loop(0, n_z, send, 0)
 
-    table_part = (0,) * 5 + (1,) * 8 + (0,) * 3
-    table_step = (0, 1, 2, 3, 4, 0, 1, 2, 3, 4, 5, 6, 7, 5, 6, 7)
-    table_ends = (0,) * 5 + (1,) * 5 + (0,) * 3 + (1,) * 3
+    early = 5
+
+    def step_of(j):
+        i = jnp.where(j < early, j, jnp.where(j < early + n_z, j - early, j - n_z))
+        return i, ((j >= early) & (j < 2 * early)) | (j >= n_z + early)
+
     keys_at, third_at, fourth_at, far_done = 0, 5, 7, 13
 
     def compute(j, _):
-        part = choose(table_part, j)
-        i = choose(table_step, j)
-        opens = choose(table_ends, j) == 0
+        part = jnp.where((j >= early) & (j < early + n_z), 1, 0)
+        i, ends = step_of(j)
+        opens = jnp.logical_not(ends)
+        before, ended = step_of(j - 2)
 
         @pl.when(j == keys_at)
         def _():
@@ -425,16 +429,16 @@
             sent_half[i] = jnp.where(c == 0, bottom, top)
             swap_half(i).start()
 
-        @pl.when((j >= 2) & (choose(table_ends, j - 2) == 1))
-        def _():
-            combine(choose(table_step, j - 2))
+        @pl.when(ended)
+        def _():
+            combine(before)
 
         return 0
 
     lax.fori_loop(0, 2 * n_z, compute, 0)
     send_keys(0)
-    combine(table_step[-2])
-    combine(table_step[-1])
+    combine(n_z - 2)
+    combine(n_z - 1)
 
     pltpu.make_async_copy(dq_in.at[pl.ds(1, n_z - 1)], dq_in.at[pl.ds(1, n_z - 1)], dq_recv).wait()
     total = own_half[0]

time: 43 us -> 42.7 us (level)
  no operation moved by 1% of the time
where the time goes in v5:
time: 42.7 us; the launch traced here: 42.6 us
  Pallas kernels  41.9 us (98%)
  between operations  0.64 us (1%)
    pallas_call x1, Pallas kernels, on_device(): pl.pallas_call(functools.partial(kernel, n_z, n_h, rows * n_s), out_shape...  40.2 us
    pallas_call x1, Pallas kernels, on_device(): pl.pallas_call(last_kernel, out_shape=(jax.ShapeDtypeStruct((HALF, tokens...  1.73 us

profile of v5, /device:TPU:1, one launch (start us, length us, event | category | flops | bytes accessed | tf_op | source)
XLA Modules:
  0.0 42.6 jit_solution(9106378290868932468)
XLA Ops:
  0.6 40.2 %shard_map.85 = (bf16[32,512]{1,0:T(8,128)(2,1)}, bf16[32,16,128]{2,1,0:T(8,128)(2,1)}) custom-call(bf16[128,4096]{1,0:T(8,128)(2,1)} %kv_hbm.1, bf16[32,512]{1,0:T(8,128)(2,1)} %q_hbm.1, bf16[32,512]{1,0:T(8,128)(2,1)} %g_hbm.1, f32[32,512]{1,0:T(8,128)} %ln_hbm.1, f32[32,512]{1,0:T(8,128)} %dl_hbm.1, s32[2]{0:T(128)} %len_hbm.1), custom_call_target="tpu_custom_call" | custom-call | flops 1342177280 | bytes 4194304 | tf_op jit(solution)/shard_map/pallas_call | solution.py:511
  40.9 1.7 %shard_map.86 = (bf16[32,512]{1,0:T(8,128)(2,1)}, bf16[128,256]{1,0:T(8,128)(2,1)}, bf16[128,256]{1,0:T(8,128)(2,1)}) custom-call(bf16[32,512]{1,0:T(8,128)(2,1)} %get-tuple-element.5.q_ref, bf16[32,16,128]{2,1,0:T(8,128)(2,1)} %get-tuple-element.6.p_ref), custom_call_target="tpu_custom_call" | custom-call | tf_op jit(solution)/shard_map/pallas_call | solution.py:560

commit v6 on v5

--- a/solution.py
+++ b/solution.py
@@ -221,16 +221,6 @@
         for way in (0, 1):
             far(way, half).start()
 
-    def send_stored(i, _):
-        pltpu.make_async_remote_copy(
-            src_ref=stored.at[z], dst_ref=stored.at[z], send_sem=stat_send, recv_sem=stat_recv,
-            device_id=(lax.rem(z + i, n_z), s), device_id_type=MESH,
-        ).start()
-        return 0
-
-    for way in (0, 1):
-        near(way).start()
-    lax.fori_loop(1, n_z, send_stored, 0)
     pair(0).start()
 
     for place in reversed(range(slots)):
@@ -241,6 +231,16 @@
         )
         unless_self(place, copy.start)
 
+    def send_stored(i, _):
+        pltpu.make_async_remote_copy(
+            src_ref=stored.at[z], dst_ref=stored.at[z], send_sem=stat_send, recv_sem=stat_recv,
+            device_id=(lax.rem(z + i, n_z), s), device_id_type=MESH,
+        ).start()
+        return 0
+
+    for way in (0, 1):
+        near(way).start()
+    lax.fori_loop(1, n_z, send_stored, 0)
     lane = lax.broadcasted_iota(jnp.int32, (LANES, DEPTH), 0)
     col = lax.broadcasted_iota(jnp.int32, (LANES, DEPTH), 1)
     side = col // PART
@@ -410,8 +410,9 @@
         q_rows = jnp.concatenate([rhs[:HALF], rhs[PART : PART + HALF], blank], 0)
         g_rows = jnp.concatenate([blank, rhs[HALF:PART], rhs[PART + HALF : 2 * PART]], 0)
         at = pl.ds(pl.multiple_of(part * chunk, chunk), chunk)
-        probs = jnp.exp(dot(lhs[0, at], rhs))
-        dscores = probs * dot(lhs[1, at], rhs)
+        both = dot(lhs[:, at].reshape(2 * chunk, DEPTH), rhs)
+        probs = jnp.exp(both[:chunk])
+        dscores = probs * both[chunk:]
         probs = probs.astype(BF16)
         dscores = dscores.astype(BF16)
         acc[at] += dot(dscores, q_rows, NT) + dot(probs, g_rows, NT)

time: 42.7 us -> 42.7 us (level)
  no operation moved by 1% of the time
where the time goes in v6:
time: 42.7 us; the launch traced here: 42.6 us
  Pallas kernels  41.9 us (98%)
  between operations  0.64 us (1%)
    pallas_call x1, Pallas kernels, on_device(): pl.pallas_call(functools.partial(kernel, n_z, n_h, rows * n_s), out_shape...  40.2 us
    pallas_call x1, Pallas kernels, on_device(): pl.pallas_call(last_kernel, out_shape=(jax.ShapeDtypeStruct((HALF, tokens...  1.73 us

profile of v6, /device:TPU:1, one launch (start us, length us, event | category | flops | bytes accessed | tf_op | source)
XLA Modules:
  0.0 42.6 jit_solution(7404530120896675903)
XLA Ops:
  0.6 40.2 %shard_map.85 = (bf16[32,512]{1,0:T(8,128)(2,1)}, bf16[32,16,128]{2,1,0:T(8,128)(2,1)}) custom-call(bf16[128,4096]{1,0:T(8,128)(2,1)} %kv_hbm.1, bf16[32,512]{1,0:T(8,128)(2,1)} %q_hbm.1, bf16[32,512]{1,0:T(8,128)(2,1)} %g_hbm.1, f32[32,512]{1,0:T(8,128)} %ln_hbm.1, f32[32,512]{1,0:T(8,128)} %dl_hbm.1, s32[2]{0:T(128)} %len_hbm.1), custom_call_target="tpu_custom_call" | custom-call | flops 1342177280 | bytes 4194304 | tf_op jit(solution)/shard_map/pallas_call | solution.py:512
  40.9 1.7 %shard_map.86 = (bf16[32,512]{1,0:T(8,128)(2,1)}, bf16[128,256]{1,0:T(8,128)(2,1)}, bf16[128,256]{1,0:T(8,128)(2,1)}) custom-call(bf16[32,512]{1,0:T(8,128)(2,1)} %get-tuple-element.5.q_ref, bf16[32,16,128]{2,1,0:T(8,128)(2,1)} %get-tuple-element.6.p_ref), custom_call_target="tpu_custom_call" | custom-call | tf_op jit(solution)/shard_map/pallas_call | solution.py:561
